TPU v7x, 32 devices: a whole 2x2x4 slice. The times are simulated.
32 devices in a mesh: row: 8 (over z, y), col: 4 (over x, core).
Axes of the slice: x: 2, y: 2, z: 4, core: 2. Of those that a mesh axis runs over, the one named last changes fastest.
Arguments:
- coords: int32 [3, 4096], P(None, ('row', 'col')), may hold values from 0 to 5376, as said below
- mode_shapes: bfloat16 [256, 4096], P(None, ('row', 'col')), as said below
- output_shapes: bfloat16 [65536, 256], P(('row', 'col')), may hold values from -0.375 to 0.375
- response_gain: float32 [2, 256], replicated, may hold values from -4 to 4
Outputs:
- response_power: float32 [65536], P(('row', 'col'))
- modal_csd: float32 [256, 256], replicated
Inputs may be any that keep to these rules, and one draw needn't show every extreme that they name: `coords`: positions of points on an aircraft's skin, numbered in no spatial order. `mode_shapes`: entries are of order 1 / sqrt(4096); each mode has a share of one sign over all nodes.
All inputs are finite; a program needn't handle non-finite values.
Results may differ from a plain program's by a relative error of at most 0.002.
Values may be sent and summed in bfloat16 or wider, within the bound.
No kernel may reach another device: no remote copies, remote signals or barrier semaphores. Data moves between devices by JAX's collectives and lax.ppermute only.
A program may use at most 64 MiB of HBM per device.

v0:
```python
import math

import jax
import jax.numpy as jnp
from jax import lax
from jax.sharding import PartitionSpec as P

wave_scale = 0.35 / 64.0


def coherence(left_points, right_points):
    difference = (left_points[:, :, None] - right_points[:, None, :]).astype(jnp.float32)
    squared = jnp.sum(difference * difference, axis=0)
    return jnp.sinc(wave_scale * jnp.sqrt(squared)).astype(jnp.bfloat16)


def split_parts(matrix):
    high_part = matrix.astype(jnp.bfloat16)
    low_part = (matrix - high_part.astype(jnp.float32)).astype(jnp.bfloat16)
    return (high_part, low_part)


def modal_product(node_shapes, node_projection):
    high_part, low_part = split_parts(node_projection)
    dims = (((1,), (1,)), ((), ()))
    upper = lax.dot_general(node_shapes, high_part, dims, preferred_element_type=jnp.float32)
    lower = lax.dot_general(node_shapes, low_part, dims, preferred_element_type=jnp.float32)
    return upper + lower


def local(coords, mode_shapes, output_shapes, response_gain):
    row_shapes, row_points = (
        lax.all_gather(mode_shapes, "col", axis=1, tiled=True),
        lax.all_gather(coords, "col", axis=1, tiled=True),
    )
    mode_count = mode_shapes.shape[0]
    zero_block = jnp.zeros((mode_count, row_points.shape[1]), jnp.float32)

    def accumulate(running, shard_piece):
        piece_shapes, piece_points = shard_piece
        length = piece_shapes.shape[1]
        block_size = math.gcd(length, 1024)
        block_count = length // block_size

        def add_block(loop_index, running_sum):
            block_start = loop_index * block_size
            part_shapes = lax.dynamic_slice_in_dim(piece_shapes, block_start, block_size, 1)
            part_points = lax.dynamic_slice_in_dim(piece_points, block_start, block_size, 1)
            coherence_tile = coherence(part_points, row_points)
            return running_sum + jnp.dot(
                part_shapes, coherence_tile, preferred_element_type=jnp.float32
            )

        if block_count == 1:
            return add_block(0, running)
        return lax.fori_loop(0, block_count, add_block, running)

    projection = accumulate(
        zero_block,
        (
            lax.all_gather(mode_shapes, "row", axis=1, tiled=True),
            lax.all_gather(coords, "row", axis=1, tiled=True),
        ),
    )
    partial_csd = modal_product(row_shapes, projection)
    modal_csd = lax.psum(partial_csd, ("row", "col"))
    real_part = response_gain[0]
    imag_part = response_gain[1]
    weighted = (
        real_part[:, None] * real_part[None, :] + imag_part[:, None] * imag_part[None, :]
    ) * modal_csd
    weighted_high, weighted_low = split_parts(weighted)
    mapped = jnp.dot(output_shapes, weighted_high, preferred_element_type=jnp.float32)
    mapped = mapped + jnp.dot(output_shapes, weighted_low, preferred_element_type=jnp.float32)
    response_power = jnp.sum(mapped * output_shapes.astype(jnp.float32), axis=1)
    return (response_power, modal_csd)


def solution(mesh):
    in_specs = (P(None, ("row", "col")), P(None, ("row", "col")), P(("row", "col"), None), P())
    out_specs = (P(("row", "col")), P())
    return jax.shard_map(local, mesh=mesh, in_specs=in_specs, out_specs=out_specs, check_vma=False)
```

profile of v0, /device:TPU:0, one launch (start us, length us, event | category | flops | bytes accessed | tf_op | source)
XLA Modules:
  0.0 213.8 jit_solution(9846555356800895200)
XLA Ops:
  7.2 0.0 all-reduce.2.cloned.1.call-start
  7.2 27.9 %all_gather.12 = s32[3,1024]{1,0:T(4,128)S(1)} all-gather(s32[3,128]{1,0:T(4,128)} %param.4), channel_id=1, replica_groups=mesh['row'=8,'col'=4] {'row'}, dimensions={1}, use_global_device_ids=true | all-gather | bytes 13824 | tf_op jit(solution)/shard_map/all_gather | solution.py:62
  35.1 5.3 %all_gather.13 = s32[3,512]{1,0:T(4,128)S(1)} all-gather(s32[3,128]{1,0:T(4,128)} %param.4), channel_id=1, replica_groups=mesh['row'=8,'col'=4] {'col'}, dimensions={1}, use_global_device_ids=true | all-gather | bytes 7680 | tf_op jit(solution)/shard_map/all_gather | solution.py:34
  40.4 27.8 %all_gather.14 = bf16[256,1024]{1,0:T(8,128)(2,1)S(1)} all-gather(bf16[256,128]{1,0:T(8,128)(2,1)} %param.5), channel_id=1, replica_groups=mesh['row'=8,'col'=4] {'row'}, dimensions={1}, use_global_device_ids=true | all-gather | bytes 589824 | tf_op jit(solution)/shard_map/all_gather | solution.py:61
  68.2 6.0 %all_gather.15 = bf16[256,512]{1,0:T(8,128)(2,1)S(1)} all-gather(bf16[256,128]{1,0:T(8,128)(2,1)} %param.5), channel_id=1, replica_groups=mesh['row'=8,'col'=4] {'col'}, dimensions={1}, use_global_device_ids=true | all-gather | bytes 327680 | tf_op jit(solution)/shard_map/all_gather | solution.py:33
  74.2 1.1 multiply_reduce_fusion
  75.4 3.1 %convolution_bitcast_fusion = f32[256,512]{0,1:T(8,128)S(1)} fusion(bf16[256,1024]{1,0:T(8,128)(2,1)S(1)} %all_gather.14, f32[1024,512]{1,0:T(8,128)S(1)} %multiply_reduce_fusion), kind=kOutput, calls=%fused_computation.29 | convolution fusion | flops 286785536 | bytes 3145728 | tf_op jit(solution)/shard_map/dot_general | solution.py:50
  78.5 0.0 copy-start
  78.5 0.3 fusion.22
  78.8 0.0 copy-start.2
  78.8 1.0 fusion.16
  79.8 0.0 all-reduce.2.cloned.1.call-update
  79.8 0.0 copy-done
  79.8 0.6 copy.8
  80.5 0.0 copy-done.2
  80.5 122.0 %all-reduce.2.cloned.1.call-done = f32[256,256]{0,1:T(8,128)} async-done(((f32[256,256]{0,1:T(8,128)}), f32[256,256]{0,1:T(8,128)}) %all-reduce.2.cloned.1.call-update) | async-done | bytes 262160 | tf_op jit(solution)/shard_map/psum | solution.py:66
  202.5 0.0 copy-start.1
  202.5 1.9 copy.9
  204.3 1.4 fusion.19
  205.8 0.0 copy-done.1
  205.8 1.2 fusion.15
  (1 shorter events, 0.0 us)
Async XLA Ops:
  7.2 195.3 %all-reduce.2.cloned.1.call-start = ((), (), s32[]{:S(2)}) async-start(), calls=%async_computation | async-start | bytes 524288 | tf_op jit(solution)/shard_map/psum | solution.py:66
  78.5 1.3 copy-start
  78.8 1.7 copy-start.2
  202.5 3.3 %copy-start.1 = (f32[256,256]{0,1:T(8,128)S(1)}, f32[256,256]{0,1:T(8,128)}, u32[]{:S(2)}) copy-start(f32[256,256]{0,1:T(8,128)} %all-reduce.2.cloned.1.call-done) | copy-start | bytes 786436
Sparse Core Ops, SparseCore 0:
  79.9 122.5 all-reduce.1
where the time goes:
time: 214 us
  waiting for transfers between devices  122 us (57%)
  blocking collectives  67 us (31%)
  between operations  14.1 us (7%)
  matrix products  6.95 us (3%)
  local copies, waits for them, and re-layouts  2.52 us (1%)
    psum x1, waiting for transfers between devices, local(): modal_csd = lax.psum(partial_csd, ('row', 'col'))  122 us
    all_gather x1, blocking collectives, local(): lax.all_gather(coords, 'row', axis=1, tiled=True)  27.9 us
    all_gather x1, blocking collectives, local(): lax.all_gather(mode_shapes, 'row', axis=1, tiled=True)  27.8 us
    all_gather x1, blocking collectives, local(): lax.all_gather(mode_shapes, 'col', axis=1, tiled=True)  6.01 us
    all_gather x1, blocking collectives, local(): lax.all_gather(coords, 'col', axis=1, tiled=True)  5.29 us
  transfers between devices with their start and end apart: 1, of which 1 were waited for; matrix products, arithmetic and copies ran while one was open for 0% of the time, Pallas kernels for 0%

commit v1 on v0

v1 whole, which is shorter than its diff:
```python
import functools
import math

import jax
import jax.numpy as jnp
from jax import lax
from jax.experimental import pallas as pl
from jax.experimental.pallas import tpu as pltpu
from jax.sharding import PartitionSpec as P

wave_scale = 0.35 / 64.0
sine_terms = (
    0.9999999970821931,
    -0.6449338560287435,
    0.1668058873098644,
    -0.023932847910373648,
    0.0021836636774330933,
    -0.00012284698513521545,
)
period_shift = 1.5 * 2.0**24
axes = ("row", "col")
POINT_ROWS = 16


def coherence(left_points, right_points):
    difference = (left_points[:, :, None] - right_points[:, None, :]).astype(jnp.float32)
    squared = jnp.sum(difference * difference, axis=0)
    return jnp.sinc(wave_scale * jnp.sqrt(squared)).astype(jnp.bfloat16)


def split_parts(matrix):
    high_part = matrix.astype(jnp.bfloat16)
    low_part = (matrix - high_part.astype(jnp.float32)).astype(jnp.bfloat16)
    return (high_part, low_part)


def modal_product(node_shapes, node_projection):
    high_part, low_part = split_parts(node_projection)
    dims = (((1,), (1,)), ((), ()))
    upper = lax.dot_general(node_shapes, high_part, dims, preferred_element_type=jnp.float32)
    lower = lax.dot_general(node_shapes, low_part, dims, preferred_element_type=jnp.float32)
    return upper + lower


def local_general(coords, mode_shapes, output_shapes, response_gain):
    row_shapes = lax.all_gather(mode_shapes, "col", axis=1, tiled=True)
    row_points = lax.all_gather(coords, "col", axis=1, tiled=True)
    mode_count = mode_shapes.shape[0]
    piece_shapes = lax.all_gather(mode_shapes, "row", axis=1, tiled=True)
    piece_points = lax.all_gather(coords, "row", axis=1, tiled=True)
    length = piece_shapes.shape[1]
    block_size = math.gcd(length, 1024)

    def add_block(loop_index, running_sum):
        block_start = loop_index * block_size
        part_shapes = lax.dynamic_slice_in_dim(piece_shapes, block_start, block_size, 1)
        part_points = lax.dynamic_slice_in_dim(piece_points, block_start, block_size, 1)
        tile = coherence(part_points, row_points)
        return running_sum + jnp.dot(part_shapes, tile, preferred_element_type=jnp.float32)

    zero_block = jnp.zeros((mode_count, row_points.shape[1]), jnp.float32)
    projection = lax.fori_loop(0, length // block_size, add_block, zero_block)
    modal_csd = lax.psum(modal_product(row_shapes, projection), axes)
    real_part, imag_part = response_gain[0], response_gain[1]
    gains = real_part[:, None] * real_part[None, :] + imag_part[:, None] * imag_part[None, :]
    weighted_high, weighted_low = split_parts(gains * modal_csd)
    mapped = jnp.dot(output_shapes, weighted_high, preferred_element_type=jnp.float32)
    mapped = mapped + jnp.dot(output_shapes, weighted_low, preferred_element_type=jnp.float32)
    response_power = jnp.sum(mapped * output_shapes.astype(jnp.float32), axis=1)
    return (response_power, modal_csd)


BIT_X, BIT_Y, BIT_Z, BIT_W = 1, 2, 4, 8


def receive(array, source):
    count = lax.axis_size(axes)
    pairs = []
    for device in range(count):
        chip, core = source(device >> 1, device & 1)
        pairs.append((chip * 2 + core, device))
    return lax.ppermute(array, axes, pairs)


def other_core(array):
    return receive(array, lambda chip, core: (chip, 1 - core))


def left_points(block):
    rows = block[256 : 256 + POINT_ROWS, :].astype(jnp.float32)
    points = rows[0:8, :] * 256.0 + rows[8:16, :]
    columns = jnp.transpose(points, (1, 0))
    return [columns[:, k : k + 1] for k in range(3)]


def right_points(block):
    rows = block[256 : 256 + POINT_ROWS, :].astype(jnp.float32)
    points = rows[0:8, :] * 256.0 + rows[8:16, :]
    return [points[k : k + 1, :] for k in range(3)]


def coherence_tile(left, right):
    squared = None
    for left_column, right_row in zip(left, right):
        difference = left_column - right_row
        term = difference * difference
        squared = term if squared is None else squared + term
    squared = jnp.maximum(squared, 1e-6)
    inverse = lax.rsqrt(squared)
    x = squared * (inverse * wave_scale)
    r = x - ((x + period_shift) - period_shift)
    z = r * r
    scale = 1.0 / wave_scale
    q = jnp.full_like(z, sine_terms[-1] * scale)
    for term in sine_terms[-2::-1]:
        q = q * z + term * scale
    return ((r * (1.0 - z)) * (q * inverse)).astype(jnp.bfloat16)


def dot(a, b):
    return jnp.dot(a, b, preferred_element_type=jnp.float32)


def dot_t(a, b):
    return lax.dot_general(a, b, (((1,), (1,)), ((), ())), preferred_element_type=jnp.float32)


def beside(*arrays):
    return jnp.concatenate(arrays, axis=1)


def shapes_of(block):
    return block[0:256, :]


def quarter(left_block, right_block):
    tile = coherence_tile(left_points(left_block), right_points(right_block))
    return dot(shapes_of(left_block), tile).astype(jnp.bfloat16), shapes_of(right_block)


def full_pair(left_halves, right_halves):
    lefts = [left_points(h) for h in left_halves]
    rights = [right_points(h) for h in right_halves]
    shapes = beside(*[shapes_of(h) for h in left_halves])
    projections = []
    for right in rights:
        column = jnp.concatenate([coherence_tile(left, right) for left in lefts], axis=0)
        projections.append(dot(shapes, column).astype(jnp.bfloat16))
    return dot_t(beside(*projections), beside(*[shapes_of(h) for h in right_halves]))


def paired(jobs):
    projections, shapes = zip(*jobs)
    return dot_t(beside(*projections), beside(*shapes))


def early_kernel(own, a, e, c_own, c_other, bits, out):
    core = bits[0]
    mine = right_points(own[0])
    total = 0.5 * dot_t(
        dot(
            beside(shapes_of(own[0]), shapes_of(own[1])),
            jnp.concatenate(
                [coherence_tile(left_points(own[0]), mine), coherence_tile(left_points(own[1]), mine)], axis=0
            ),
        ).astype(jnp.bfloat16),
        shapes_of(own[0]),
    )
    u = bits[1]
    jobs = []
    for k in range(2):
        left_half, right_half = u * k, u | k
        jobs.append(quarter(own[left_half ^ core], a[right_half ^ core]))
    total += paired(jobs)
    u = bits[2]
    left_half = jnp.where(u == 1, 1, core)
    right_half = jnp.where(u == 1, core, 0)
    projection, shapes = quarter(e[left_half ^ (1 - core)], a[right_half ^ core])
    total += dot_t(projection, shapes)
    total += full_pair([a[0], a[1]], [c_own[...], c_other[...]])
    out[...] = total


def late_kernel(own, a, b, e, c_own, c_other, bits, early, out):
    core = bits[0]
    u = bits[3]
    total = early[...]
    jobs = []
    for k in range(2):
        left_half, right_half = u * k, u | k
        jobs.append(quarter(own[left_half ^ core], b[right_half ^ core]))
    total += paired(jobs)
    left_half = jnp.where(u == 1, 1, core)
    right_half = jnp.where(u == 1, core, 0)
    right = b[right_half ^ core]
    total += paired([quarter(a[left_half ^ core], right), quarter(e[left_half ^ (1 - core)], right)])
    total += full_pair([b[0], b[1]], [c_own[...], c_other[...]])
    first = total[0:128, 0:128] + total[0:128, 0:128].T
    second = total[128:256, 128:256] + total[128:256, 128:256].T
    cross = total[0:128, 128:256] + total[128:256, 0:128].T
    r = lax.broadcasted_iota(jnp.int32, (128, 128), 0)
    s = lax.broadcasted_iota(jnp.int32, (128, 128), 1)
    out[0:128, 0:128] = jnp.where(r <= s, first, second)
    out[0:128, 128:256] = cross
    diagonal = jnp.sum(jnp.where(r == s, second, 0.0), axis=0, keepdims=True)
    out[128:144, :] = jnp.broadcast_to(beside(diagonal, diagonal), (16, 256))


def answer_kernel(own, pa, pb, pc, gains, outputs_t, power, csd):
    packed = (own[...] + pa[...]) + (pb[...] + pc[...])
    r = lax.broadcasted_iota(jnp.int32, (128, 128), 0)
    s = lax.broadcasted_iota(jnp.int32, (128, 128), 1)
    corner = packed[0:128, 0:128]
    turned = corner.T
    diagonal = packed[128:129, 0:128]
    first = jnp.where(r <= s, corner, turned)
    second = jnp.where(r > s, corner, jnp.where(r == s, diagonal, turned))
    cross = packed[0:128, 128:256]
    whole = jnp.concatenate([beside(first, cross), beside(cross.T, second)], axis=0)
    csd[...] = whole
    g = gains[...]
    columns = jnp.transpose(g, (1, 0))
    weight = columns[:, 0:1] * g[0:1, :] + columns[:, 1:2] * g[1:2, :]
    weighted = (weight * whole).astype(jnp.bfloat16)
    width = 512
    for k in range(outputs_t.shape[1] // width):
        part = outputs_t[:, k * width : (k + 1) * width]
        mapped = dot(weighted, part)
        power[:, k * width : (k + 1) * width] = jnp.sum(mapped * part.astype(jnp.float32), axis=0, keepdims=True)


VMEM = pl.BlockSpec(memory_space=pltpu.VMEM)
SMEM = pl.BlockSpec(memory_space=pltpu.SMEM)


def call(kernel, specs, outs, *operands):
    return pl.pallas_call(
        kernel,
        in_specs=specs,
        out_specs=[VMEM] * len(outs) if len(outs) > 1 else VMEM,
        out_shape=outs if len(outs) > 1 else outs[0],
        compiler_params=pltpu.CompilerParams(vmem_limit_bytes=24 * 2**20),
    )(*operands)


def four_chips(packed, first, second, kind):
    core = lax.axis_index("col") & 1
    sent = packed.astype(kind)
    half = sent.shape[0] // 2
    far = receive(sent, lambda chip, c: (chip ^ (second if c == 0 else first ^ second), c))
    part = lax.dynamic_slice_in_dim(sent, core * half, half, 0)
    near = receive(part, lambda chip, c: (chip ^ first, c))
    far_other = other_core(far)
    near_other = other_core(near)
    near_all = jnp.where(
        core == 0,
        jnp.concatenate([near, near_other], axis=0),
        jnp.concatenate([near_other, near], axis=0),
    )
    return sent, near_all, far, far_other


def local_chips(coords, mode_shapes, output_shapes, response_gain):
    row, col = lax.axis_index("row"), lax.axis_index("col")
    core = col & 1
    x, y, z = col >> 1, row & 1, (row >> 1) & 1
    bits = jnp.stack(
        [
            core,
            jnp.where(core == 0, x, y),
            jnp.where(core == 0, 1 - y, y),
            z,
        ]
    ).astype(jnp.int32)
    blank = jnp.zeros((5, coords.shape[1]), jnp.bfloat16)
    high = (coords >> 8).astype(jnp.bfloat16)
    low = (coords & 255).astype(jnp.bfloat16)
    packed = jnp.concatenate([mode_shapes, high, blank, low, blank], axis=0)
    c_own = receive(packed, lambda chip, c: (chip ^ (BIT_W if chip < BIT_W else BIT_W | BIT_Z), c))
    own = jnp.stack([packed, other_core(packed)])
    a = receive(own, lambda chip, c: (chip ^ (BIT_X if c == 0 else BIT_Y), c))
    b = receive(own, lambda chip, c: (chip ^ (BIT_Z if c == 0 else BIT_X | BIT_Y | BIT_Z), c))
    c_other = other_core(c_own)
    e = other_core(a)
    modes = mode_shapes.shape[0]
    square = jax.ShapeDtypeStruct((modes, modes), jnp.float32)
    tri = jax.ShapeDtypeStruct((modes // 2 + 16, modes), jnp.float32)
    early = call(early_kernel, [VMEM] * 5 + [SMEM], [square], own, a, e, c_own, c_other, bits)
    mine = call(late_kernel, [VMEM] * 6 + [SMEM, VMEM], [tri], own, a, b, e, c_own, c_other, bits, early)
    chip_sum = mine + other_core(mine)
    s, pa, pb, pc = four_chips(chip_sum, BIT_Z, BIT_W, jnp.bfloat16)
    f = jnp.float32
    line_sum = (s.astype(f) + pa.astype(f)) + (pb.astype(f) + pc.astype(f))
    s, pa, pb, pc = four_chips(line_sum, BIT_X, BIT_Y, jnp.float32)
    count = output_shapes.shape[0]
    power, csd = call(
        answer_kernel,
        [VMEM] * 6,
        [jax.ShapeDtypeStruct((1, count), jnp.float32), square],
        s,
        pa,
        pb,
        pc,
        response_gain,
        output_shapes.T,
    )
    return (power.reshape(count), csd)


def solution(mesh):
    in_specs = (P(None, axes), P(None, axes), P(axes, None), P())
    out_specs = (P(axes), P())

    def whole(coords, mode_shapes, output_shapes, response_gain):
        shape = (mode_shapes.shape[0], mode_shapes.shape[1] // mesh.size)
        chips = mesh.shape["row"] == 8 and mesh.shape["col"] == 4 and shape == (256, 128)
        local = local_chips if chips else local_general
        return jax.shard_map(local, mesh=mesh, in_specs=in_specs, out_specs=out_specs, check_vma=False)(
            coords, mode_shapes, output_shapes, response_gain
        )

    return whole
```

time: 214 us -> 39.2 us (0.18)
  waiting for transfers between devices: 122 us -> 13.3 us
  blocking collectives: 67 us -> 0 us
  starting transfers between devices: 0.04 us -> 17.1 us
  between operations: 14.1 us -> 0.7 us
  matrix products: 6.95 us -> 0 us
  Pallas kernels: 0 us -> 5.05 us
    psum x1 -> x0, waiting for transfers between devices: 122 us -> none  [local(): modal_csd = lax.psum(partial_csd, ('row', 'col'))]
    all_gather x4 -> x0, blocking collectives: 67 us -> none  [the longest x1 27.9 us: local(): lax.all_gather(coords, 'row', axis=1, tiled=True)]
    ppermute x0 -> x15, starting transfers between devices: none -> 17.1 us  [receive(): return lax.ppermute(array, axes, pairs)]
    ppermute x0 -> x15, waiting for transfers between devices: none -> 13.3 us  [receive(): return lax.ppermute(array, axes, pairs)]
    dot_general x5 -> x0, matrix products: 6.95 us -> none  [the longest x1 3.09 us: add_block(): jnp.dot(part_shapes, coherence_tile, preferred_element_type=jnp.float32)]
    pallas_call x0 -> x3, Pallas kernels: none -> 5.05 us  [call(): pl.pallas_call(kernel, in_specs=specs, out_specs=[VMEM] * len(outs) if le...]
  transfers between devices with their start and end apart: 1 -> 15, of which waited for: 1 -> 10; matrix products, arithmetic and copies ran while one was open for 0% -> 2% of each run, Pallas kernels for 0% -> 5%
where the time goes in v1:
time: 39.2 us; the launch traced here: 39 us
  starting transfers between devices  17.1 us (44%)
  waiting for transfers between devices  13.3 us (34%)
  Pallas kernels  5.05 us (13%)
  local copies, waits for them, and re-layouts  1.9 us (5%)
  other arithmetic  0.86 us (2%)
  between operations  0.7 us (2%)
    ppermute x15, starting transfers between devices, receive(): return lax.ppermute(array, axes, pairs)  17.1 us
    ppermute x15, waiting for transfers between devices, receive(): return lax.ppermute(array, axes, pairs)  13.3 us
    pallas_call x3, Pallas kernels, call(): pl.pallas_call(kernel, in_specs=specs, out_specs=[VMEM] * len(outs) if le...  5.05 us
    unnamed x5, local copies, waits for them, and re-layouts  0.98 us
    concatenate x1, local copies, waits for them, and re-layouts, local_chips(): packed = jnp.concatenate([mode_shapes, high, blank, low, blank], axis=0)  0.91 us
  transfers between devices with their start and end apart: 15, of which 10 were waited for; matrix products, arithmetic and copies ran while one was open for 2% of the time, Pallas kernels for 5%

profile of v1, /device:TPU:0, one launch (start us, length us, event | category | flops | bytes accessed | tf_op | source)
XLA Modules:
  0.0 39.0 jit_solution(12067162537551774095)
XLA Ops:
  0.6 0.7 %and_convert_fusion = (bf16[3,128]{1,0:T(4,128)(2,1)S(1)}, bf16[3,128]{1,0:T(4,128)(2,1)S(1)}) fusion(s32[3,128]{1,0:T(4,128)} %param.4), kind=kLoop, calls=%fused_computation.5 | loop fusion | flops 1536 | bytes 3072 | tf_op jit(solution)/shard_map/convert_element_type | solution.py:277
  1.3 0.9 %concatenate.15 = bf16[272,128]{1,0:T(8,128)(2,1)S(1)} concatenate(bf16[256,128]{1,0:T(8,128)(2,1)} %param.5, bf16[3,128]{1,0:T(4,128)(2,1)S(1)} %get-tuple-element.7, bf16[5,128]{1,0:T(8,128)(2,1)S(1)} %broadcast_in_dim.3, bf16[3,128]{1,0:T(4,128)(2,1)S(1)} %get-tuple-element.6, bf16[5,128]{1,0:T(8,128)(2,1)S(1)} %broadcast_in_dim.3), dimensions={0} | concatenate | bytes 139264 | tf_op jit(solution)/shard_map/concatenate | solution.py:278
  2.2 0.5 %collective-permute-start = (bf16[272,128]{1,0:T(8,128)(2,1)S(1)}, bf16[272,128]{1,0:T(8,128)(2,1)S(1)}, u32[]{:S(2)}, u32[]{:S(2)}) collective-permute-start(bf16[272,128]{1,0:T(8,128)(2,1)S(1)} %concatenate.15), channel_id=1, source_target_pairs={{1,0},{0,1},{3,2},{2,3},{5,4},{4,5},{7,6},{6,7},{9,8},{8,9},{11,10... | collective-permute-start | bytes 208904 | tf_op jit(solution)/shard_map/ppermute | solution.py:82
  2.7 0.9 %collective-permute-done = bf16[272,128]{1,0:T(8,128)(2,1)S(1)} collective-permute-done((bf16[272,128]{1,0:T(8,128)(2,1)S(1)}, bf16[272,128]{1,0:T(8,128)(2,1)S(1)}, u32[]{:S(2)}, u32[]{:S(2)}) %collective-permute-start) | collective-permute-done | bytes 69664 | tf_op jit(solution)/shard_map/ppermute | solution.py:82
  3.7 2.9 %collective-permute-start.1 = (bf16[2,272,128]{2,1,0:T(8,128)(2,1)S(1)}, bf16[2,272,128]{2,1,0:T(8,128)(2,1)S(1)}, u32[]{:S(2)}, u32[]{:S(2)}) collective-permute-start(bf16[2,272,128]{2,1,0:T(8,128)(2,1)S(1)} %pad_maximum_fusion.own), channel_id=1, source_target_pairs={{2,0},{5,1},{0,2},{7,3},{6,4},{1,5},{4,6},{3,7},{10,8},{13,9},{8,1... | collective-permute-start | bytes 417800 | tf_op jit(solution)/shard_map/ppermute | solution.py:82
  6.6 3.6 %collective-permute-start.4 = (bf16[272,128]{1,0:T(8,128)(2,1)S(1)}, bf16[272,128]{1,0:T(8,128)(2,1)S(1)}, u32[]{:S(2)}, u32[]{:S(2)}) collective-permute-start(bf16[272,128]{1,0:T(8,128)(2,1)S(1)} %concatenate.15), channel_id=1, source_target_pairs={{16,0},{17,1},{18,2},{19,3},{20,4},{21,5},{22,6},{23,7},{24,8},{25... | collective-permute-start | bytes 208904 | tf_op jit(solution)/shard_map/ppermute | solution.py:82
  10.2 1.5 %collective-permute-start.2 = (bf16[2,272,128]{2,1,0:T(8,128)(2,1)S(1)}, bf16[2,272,128]{2,1,0:T(8,128)(2,1)S(1)}, u32[]{:S(2)}, u32[]{:S(2)}) collective-permute-start(bf16[2,272,128]{2,1,0:T(8,128)(2,1)S(1)} %pad_maximum_fusion.own), channel_id=1, source_target_pairs={{8,0},{15,1},{10,2},{13,3},{12,4},{11,5},{14,6},{9,7},{0,8},{7,9},... | collective-permute-start | bytes 417800 | tf_op jit(solution)/shard_map/ppermute | solution.py:82
  11.7 1.5 %collective-permute-done.4.c_own = bf16[272,128]{1,0:T(8,128)(2,1)S(1)} collective-permute-done((bf16[272,128]{1,0:T(8,128)(2,1)S(1)}, bf16[272,128]{1,0:T(8,128)(2,1)S(1)}, u32[]{:S(2)}, u32[]{:S(2)}) %collective-permute-start.4) | collective-permute-done | bytes 69664 | tf_op jit(solution)/shard_map/ppermute | solution.py:82
  13.2 0.6 %collective-permute-start.5 = (bf16[272,128]{1,0:T(8,128)(2,1)S(1)}, bf16[272,128]{1,0:T(8,128)(2,1)S(1)}, u32[]{:S(2)}, u32[]{:S(2)}) collective-permute-start(bf16[272,128]{1,0:T(8,128)(2,1)S(1)} %collective-permute-done.4.c_own), channel_id=1, source_target_pairs={{1,0},{0,1},{3,2},{2,3},{5,4},{4,5},{7,6},{6,7},{9,8},{8,9},{11,10... | collective-permute-start | bytes 208904 | tf_op jit(solution)/shard_map/ppermute | solution.py:82
  13.9 0.8 %collective-permute-done.5.c_other = bf16[272,128]{1,0:T(8,128)(2,1)S(1)} collective-permute-done((bf16[272,128]{1,0:T(8,128)(2,1)S(1)}, bf16[272,128]{1,0:T(8,128)(2,1)S(1)}, u32[]{:S(2)}, u32[]{:S(2)}) %collective-permute-start.5) | collective-permute-done | bytes 69664 | tf_op jit(solution)/shard_map/ppermute | solution.py:82
  14.7 2.0 %shard_map.59.early = f32[256,256]{1,0:T(8,128)S(1)} custom-call(bf16[2,272,128]{2,1,0:T(8,128)(2,1)S(1)} %pad_maximum_fusion.own, bf16[2,272,128]{2,1,0:T(8,128)(2,1)S(1)} %collective-permute-done.1.a, bf16[2,272,128]{2,1,0:T(8,128)(2,1)S(1)} %collective-permute-done.3.e, bf16[272,128]{1,0:T(8,128)(2,1)S(1)} %collective-permute-done.4.c_own, ...), custom_call_target="tpu_custom_call" | custom-call | tf_op jit(solution)/shard_map/pallas_call | solution.py:237
  16.7 1.8 %shard_map.60 = f32[144,256]{1,0:T(8,128)S(1)} custom-call(bf16[2,272,128]{2,1,0:T(8,128)(2,1)S(1)} %pad_maximum_fusion.own, bf16[2,272,128]{2,1,0:T(8,128)(2,1)S(1)} %collective-permute-done.1.a, bf16[2,272,128]{2,1,0:T(8,128)(2,1)S(1)} %collective-permute-done.2.b, bf16[2,272,128]{2,1,0:T(8,128)(2,1)S(1)} %collective-permute-done.3.e, ...), custom_call_target="tpu_custom_call" | custom-call | tf_op jit(solution)/shard_map/pallas_call | solution.py:237
  18.5 0.8 %collective-permute-start.6 = (f32[144,256]{1,0:T(8,128)S(1)}, f32[144,256]{1,0:T(8,128)S(1)}, u32[]{:S(2)}, u32[]{:S(2)}) collective-permute-start(f32[144,256]{1,0:T(8,128)S(1)} %shard_map.60), channel_id=1, source_target_pairs={{1,0},{0,1},{3,2},{2,3},{5,4},{4,5},{7,6},{6,7},{9,8},{8,9},{11,10... | collective-permute-start | bytes 442376 | tf_op jit(solution)/shard_map/ppermute | solution.py:82
  19.3 1.0 %collective-permute-done.6 = f32[144,256]{1,0:T(8,128)S(1)} collective-permute-done((f32[144,256]{1,0:T(8,128)S(1)}, f32[144,256]{1,0:T(8,128)S(1)}, u32[]{:S(2)}, u32[]{:S(2)}) %collective-permute-start.6) | collective-permute-done | bytes 147488 | tf_op jit(solution)/shard_map/ppermute | solution.py:82
  20.3 2.6 %collective-permute-start.9 = (bf16[144,256]{1,0:T(8,128)(2,1)S(1)}, bf16[144,256]{1,0:T(8,128)(2,1)S(1)}, u32[]{:S(2)}, u32[]{:S(2)}) collective-permute-start(bf16[144,256]{1,0:T(8,128)(2,1)S(1)} %add_convert_fusion), channel_id=1, source_target_pairs={{16,0},{25,1},{18,2},{27,3},{20,4},{29,5},{22,6},{31,7},{24,8},{17... | collective-permute-start | bytes 221192 | tf_op jit(solution)/shard_map/ppermute | solution.py:82
  22.9 1.6 %collective-permute-start.7 = (bf16[72,256]{1,0:T(8,128)(2,1)S(1)}, bf16[72,256]{1,0:T(8,128)(2,1)S(1)}, u32[]{:S(2)}, u32[]{:S(2)}) collective-permute-start(bf16[72,256]{1,0:T(8,128)(2,1)S(1)} %constant_dynamic-slice_fusion.1), channel_id=1, source_target_pairs={{8,0},{9,1},{10,2},{11,3},{12,4},{13,5},{14,6},{15,7},{0,8},{1,9},... | collective-permute-start | bytes 110600 | tf_op jit(solution)/shard_map/ppermute | solution.py:82
  24.5 3.1 %collective-permute-done.9 = bf16[144,256]{1,0:T(8,128)(2,1)S(1)} collective-permute-done((bf16[144,256]{1,0:T(8,128)(2,1)S(1)}, bf16[144,256]{1,0:T(8,128)(2,1)S(1)}, u32[]{:S(2)}, u32[]{:S(2)}) %collective-permute-start.9) | collective-permute-done | bytes 73760 | tf_op jit(solution)/shard_map/ppermute | solution.py:82
  27.7 0.4 collective-permute-start.8
  28.1 0.9 %collective-permute-done.8 = bf16[72,256]{1,0:T(8,128)(2,1)S(1)} collective-permute-done((bf16[72,256]{1,0:T(8,128)(2,1)S(1)}, bf16[72,256]{1,0:T(8,128)(2,1)S(1)}, u32[]{:S(2)}, u32[]{:S(2)}) %collective-permute-start.8) | collective-permute-done | bytes 36896 | tf_op jit(solution)/shard_map/ppermute | solution.py:82
  29.0 1.6 %collective-permute-start.13 = (f32[144,256]{1,0:T(8,128)S(1)}, f32[144,256]{1,0:T(8,128)S(1)}, u32[]{:S(2)}, u32[]{:S(2)}) collective-permute-start(f32[144,256]{1,0:T(8,128)S(1)} %add_add_fusion.own), channel_id=1, source_target_pairs={{4,0},{7,1},{6,2},{5,3},{0,4},{3,5},{2,6},{1,7},{12,8},{15,9},{14,... | collective-permute-start | bytes 442376 | tf_op jit(solution)/shard_map/ppermute | solution.py:82
  30.6 0.6 %collective-permute-start.11 = (f32[72,256]{1,0:T(8,128)S(1)}, f32[72,256]{1,0:T(8,128)S(1)}, u32[]{:S(2)}, u32[]{:S(2)}) collective-permute-start(f32[72,256]{1,0:T(8,128)S(1)} %constant_dynamic-slice_fusion), channel_id=1, source_target_pairs={{2,0},{3,1},{0,2},{1,3},{6,4},{7,5},{4,6},{5,7},{10,8},{11,9},{8,1... | collective-permute-start | bytes 221192 | tf_op jit(solution)/shard_map/ppermute | solution.py:82
  31.2 4.6 %collective-permute-done.11 = f32[72,256]{1,0:T(8,128)S(1)} collective-permute-done((f32[72,256]{1,0:T(8,128)S(1)}, f32[72,256]{1,0:T(8,128)S(1)}, u32[]{:S(2)}, u32[]{:S(2)}) %collective-permute-start.11) | collective-permute-done | bytes 73760 | tf_op jit(solution)/shard_map/ppermute | solution.py:82
  36.3 0.6 %copy.6 = bf16[2048,256]{0,1:T(8,128)(2,1)S(1)} copy(bf16[2048,256]{1,0:T(8,128)(2,1)S(1)} %copy-done.1) | data formatting | bytes 2097152 | tf_op args[2]
  37.7 1.3 %shard_map.61 = (f32[1,2048]{1,0:T(1,128)}, f32[256,256]{1,0:T(8,128)}) custom-call(f32[144,256]{1,0:T(8,128)S(1)} %add_add_fusion.own, f32[144,256]{1,0:T(8,128)S(1)} %maximum_select_fusion.pa, f32[144,256]{1,0:T(8,128)S(1)} %collective-permute-done.13.pb, f32[144,256]{1,0:T(8,128)S(1)} %collective-permute-done.14.pc, f32[2,256]{1,0:T(2,128)S(1)} %copy-done, ...), custom_call_target="tpu_custom_call" | custom-call | tf_op jit(solution)/shard_map/pallas_call | solution.py:237
  (24 shorter events, 1.6 us)
Async XLA Ops:
  2.2 1.4 %collective-permute-start = (bf16[272,128]{1,0:T(8,128)(2,1)S(1)}, bf16[272,128]{1,0:T(8,128)(2,1)S(1)}, u32[]{:S(2)}, u32[]{:S(2)}) collective-permute-start(bf16[272,128]{1,0:T(8,128)(2,1)S(1)} %concatenate.15), channel_id=1, source_target_pairs={{1,0},{0,1},{3,2},{2,3},{5,4},{4,5},{7,6},{6,7},{9,8},{8,9},{11,10... | collective-permute-start | bytes 208904 | tf_op jit(solution)/shard_map/ppermute | solution.py:82
  3.7 6.5 %collective-permute-start.1 = (bf16[2,272,128]{2,1,0:T(8,128)(2,1)S(1)}, bf16[2,272,128]{2,1,0:T(8,128)(2,1)S(1)}, u32[]{:S(2)}, u32[]{:S(2)}) collective-permute-start(bf16[2,272,128]{2,1,0:T(8,128)(2,1)S(1)} %pad_maximum_fusion.own), channel_id=1, source_target_pairs={{2,0},{5,1},{0,2},{7,3},{6,4},{1,5},{4,6},{3,7},{10,8},{13,9},{8,1... | collective-permute-start | bytes 417800 | tf_op jit(solution)/shard_map/ppermute | solution.py:82
  6.6 6.6 %collective-permute-start.4 = (bf16[272,128]{1,0:T(8,128)(2,1)S(1)}, bf16[272,128]{1,0:T(8,128)(2,1)S(1)}, u32[]{:S(2)}, u32[]{:S(2)}) collective-permute-start(bf16[272,128]{1,0:T(8,128)(2,1)S(1)} %concatenate.15), channel_id=1, source_target_pairs={{16,0},{17,1},{18,2},{19,3},{20,4},{21,5},{22,6},{23,7},{24,8},{25... | collective-permute-start | bytes 208904 | tf_op jit(solution)/shard_map/ppermute | solution.py:82
  10.2 4.6 %collective-permute-start.3 = (bf16[2,272,128]{2,1,0:T(8,128)(2,1)S(1)}, bf16[2,272,128]{2,1,0:T(8,128)(2,1)S(1)}, u32[]{:S(2)}, u32[]{:S(2)}) collective-permute-start(bf16[2,272,128]{2,1,0:T(8,128)(2,1)S(1)} %collective-permute-done.1.a), channel_id=1, source_target_pairs={{1,0},{0,1},{3,2},{2,3},{5,4},{4,5},{7,6},{6,7},{9,8},{8,9},{11,10... | collective-permute-start | bytes 417800 | tf_op jit(solution)/shard_map/ppermute | solution.py:82
  10.2 6.6 %collective-permute-start.2 = (bf16[2,272,128]{2,1,0:T(8,128)(2,1)S(1)}, bf16[2,272,128]{2,1,0:T(8,128)(2,1)S(1)}, u32[]{:S(2)}, u32[]{:S(2)}) collective-permute-start(bf16[2,272,128]{2,1,0:T(8,128)(2,1)S(1)} %pad_maximum_fusion.own), channel_id=1, source_target_pairs={{8,0},{15,1},{10,2},{13,3},{12,4},{11,5},{14,6},{9,7},{0,8},{7,9},... | collective-permute-start | bytes 417800 | tf_op jit(solution)/shard_map/ppermute | solution.py:82
  13.2 1.5 %collective-permute-start.5 = (bf16[272,128]{1,0:T(8,128)(2,1)S(1)}, bf16[272,128]{1,0:T(8,128)(2,1)S(1)}, u32[]{:S(2)}, u32[]{:S(2)}) collective-permute-start(bf16[272,128]{1,0:T(8,128)(2,1)S(1)} %collective-permute-done.4.c_own), channel_id=1, source_target_pairs={{1,0},{0,1},{3,2},{2,3},{5,4},{4,5},{7,6},{6,7},{9,8},{8,9},{11,10... | collective-permute-start | bytes 208904 | tf_op jit(solution)/shard_map/ppermute | solution.py:82
  16.7 19.6 %copy-start.1 = (bf16[2048,256]{1,0:T(8,128)(2,1)S(1)}, bf16[2048,256]{1,0:T(8,128)(2,1)}, u32[]{:S(2)}) copy-start(bf16[2048,256]{1,0:T(8,128)(2,1)} %param.6) | copy-start | bytes 3145732
  18.5 1.8 %collective-permute-start.6 = (f32[144,256]{1,0:T(8,128)S(1)}, f32[144,256]{1,0:T(8,128)S(1)}, u32[]{:S(2)}, u32[]{:S(2)}) collective-permute-start(f32[144,256]{1,0:T(8,128)S(1)} %shard_map.60), channel_id=1, source_target_pairs={{1,0},{0,1},{3,2},{2,3},{5,4},{4,5},{7,6},{6,7},{9,8},{8,9},{11,10... | collective-permute-start | bytes 442376 | tf_op jit(solution)/shard_map/ppermute | solution.py:82
  20.3 7.2 %collective-permute-start.9 = (bf16[144,256]{1,0:T(8,128)(2,1)S(1)}, bf16[144,256]{1,0:T(8,128)(2,1)S(1)}, u32[]{:S(2)}, u32[]{:S(2)}) collective-permute-start(bf16[144,256]{1,0:T(8,128)(2,1)S(1)} %add_convert_fusion), channel_id=1, source_target_pairs={{16,0},{25,1},{18,2},{27,3},{20,4},{29,5},{22,6},{31,7},{24,8},{17... | collective-permute-start | bytes 221192 | tf_op jit(solution)/shard_map/ppermute | solution.py:82
  22.9 4.8 %collective-permute-start.7 = (bf16[72,256]{1,0:T(8,128)(2,1)S(1)}, bf16[72,256]{1,0:T(8,128)(2,1)S(1)}, u32[]{:S(2)}, u32[]{:S(2)}) collective-permute-start(bf16[72,256]{1,0:T(8,128)(2,1)S(1)} %constant_dynamic-slice_fusion.1), channel_id=1, source_target_pairs={{8,0},{9,1},{10,2},{11,3},{12,4},{13,5},{14,6},{15,7},{0,8},{1,9},... | collective-permute-start | bytes 110600 | tf_op jit(solution)/shard_map/ppermute | solution.py:82
  27.5 1.4 %collective-permute-start.10 = (bf16[144,256]{1,0:T(8,128)(2,1)S(1)}, bf16[144,256]{1,0:T(8,128)(2,1)S(1)}, u32[]{:S(2)}, u32[]{:S(2)}) collective-permute-start(bf16[144,256]{1,0:T(8,128)(2,1)S(1)} %collective-permute-done.9), channel_id=1, source_target_pairs={{1,0},{0,1},{3,2},{2,3},{5,4},{4,5},{7,6},{6,7},{9,8},{8,9},{11,10... | collective-permute-start | bytes 221192 | tf_op jit(solution)/shard_map/ppermute | solution.py:82
  27.7 1.2 %collective-permute-start.8 = (bf16[72,256]{1,0:T(8,128)(2,1)S(1)}, bf16[72,256]{1,0:T(8,128)(2,1)S(1)}, u32[]{:S(2)}, u32[]{:S(2)}) collective-permute-start(bf16[72,256]{1,0:T(8,128)(2,1)S(1)} %collective-permute-done.7), channel_id=1, source_target_pairs={{1,0},{0,1},{3,2},{2,3},{5,4},{4,5},{7,6},{6,7},{9,8},{8,9},{11,10... | collective-permute-start | bytes 110600 | tf_op jit(solution)/shard_map/ppermute | solution.py:82
  29.0 7.0 %collective-permute-start.13 = (f32[144,256]{1,0:T(8,128)S(1)}, f32[144,256]{1,0:T(8,128)S(1)}, u32[]{:S(2)}, u32[]{:S(2)}) collective-permute-start(f32[144,256]{1,0:T(8,128)S(1)} %add_add_fusion.own), channel_id=1, source_target_pairs={{4,0},{7,1},{6,2},{5,3},{0,4},{3,5},{2,6},{1,7},{12,8},{15,9},{14,... | collective-permute-start | bytes 442376 | tf_op jit(solution)/shard_map/ppermute | solution.py:82
  30.6 5.2 %collective-permute-start.11 = (f32[72,256]{1,0:T(8,128)S(1)}, f32[72,256]{1,0:T(8,128)S(1)}, u32[]{:S(2)}, u32[]{:S(2)}) collective-permute-start(f32[72,256]{1,0:T(8,128)S(1)} %constant_dynamic-slice_fusion), channel_id=1, source_target_pairs={{2,0},{3,1},{0,2},{1,3},{6,4},{7,5},{4,6},{5,7},{10,8},{11,9},{8,1... | collective-permute-start | bytes 221192 | tf_op jit(solution)/shard_map/ppermute | solution.py:82
  35.7 1.3 %collective-permute-start.12 = (f32[72,256]{1,0:T(8,128)S(1)}, f32[72,256]{1,0:T(8,128)S(1)}, u32[]{:S(2)}, u32[]{:S(2)}) collective-permute-start(f32[72,256]{1,0:T(8,128)S(1)} %collective-permute-done.11), channel_id=1, source_target_pairs={{1,0},{0,1},{3,2},{2,3},{5,4},{4,5},{7,6},{6,7},{9,8},{8,9},{11,10... | collective-permute-start | bytes 221192 | tf_op jit(solution)/shard_map/ppermute | solution.py:82
  36.0 1.4 %collective-permute-start.14 = (f32[144,256]{1,0:T(8,128)S(1)}, f32[144,256]{1,0:T(8,128)S(1)}, u32[]{:S(2)}, u32[]{:S(2)}) collective-permute-start(f32[144,256]{1,0:T(8,128)S(1)} %collective-permute-done.13.pb), channel_id=1, source_target_pairs={{1,0},{0,1},{3,2},{2,3},{5,4},{4,5},{7,6},{6,7},{9,8},{8,9},{11,10... | collective-permute-start | bytes 442376 | tf_op jit(solution)/shard_map/ppermute | solution.py:82
  37.0 0.7 %copy-start = (f32[2,256]{1,0:T(2,128)S(1)}, f32[2,256]{1,0:T(2,128)}, u32[]{:S(2)}) copy-start(f32[2,256]{1,0:T(2,128)} %gains.1) | copy-start | bytes 6148

commit v2 on v1

--- a/solution.py
+++ b/solution.py
@@ -20,6 +20,7 @@
 period_shift = 1.5 * 2.0**24
 axes = ("row", "col")
 POINT_ROWS = 16
+BOUND_ROW = 136
 
 
 def coherence(left_points, right_points):
@@ -154,8 +155,14 @@
     return dot_t(beside(*projections), beside(*shapes))
 
 
-def early_kernel(own, a, e, c_own, c_other, bits, out):
-    core = bits[0]
+def place():
+    row, col = lax.axis_index("row"), lax.axis_index("col")
+    return col & 1, col >> 1, row & 1, (row >> 1) & 1
+
+
+def early_kernel(own, a, e, c_own, c_other, response_gain, out, gains):
+    gains[...] = response_gain[...]
+    core, x, y, _ = place()
     mine = right_points(own[0])
     total = 0.5 * dot_t(
         dot(
@@ -166,13 +173,13 @@
         ).astype(jnp.bfloat16),
         shapes_of(own[0]),
     )
-    u = bits[1]
+    u = jnp.where(core == 0, x, y)
     jobs = []
     for k in range(2):
         left_half, right_half = u * k, u | k
         jobs.append(quarter(own[left_half ^ core], a[right_half ^ core]))
     total += paired(jobs)
-    u = bits[2]
+    u = jnp.where(core == 0, 1 - y, y)
     left_half = jnp.where(u == 1, 1, core)
     right_half = jnp.where(u == 1, core, 0)
     projection, shapes = quarter(e[left_half ^ (1 - core)], a[right_half ^ core])
@@ -181,9 +188,8 @@
     out[...] = total
 
 
-def late_kernel(own, a, b, e, c_own, c_other, bits, early, out):
-    core = bits[0]
-    u = bits[3]
+def late_kernel(own, a, b, e, c_own, c_other, early, out):
+    core, _, _, u = place()
     total = early[...]
     jobs = []
     for k in range(2):
@@ -203,11 +209,14 @@
     out[0:128, 0:128] = jnp.where(r <= s, first, second)
     out[0:128, 128:256] = cross
     diagonal = jnp.sum(jnp.where(r == s, second, 0.0), axis=0, keepdims=True)
-    out[128:144, :] = jnp.broadcast_to(beside(diagonal, diagonal), (16, 256))
-
-
-def answer_kernel(own, pa, pb, pc, gains, outputs_t, power, csd):
-    packed = (own[...] + pa[...]) + (pb[...] + pc[...])
+    out[128:BOUND_ROW, :] = jnp.broadcast_to(beside(diagonal, diagonal), (8, 256))
+    largest = jnp.maximum(jnp.abs(out[0:128, :]), jnp.abs(out[128:129, :]))
+    largest = jnp.max(jnp.max(largest, axis=0, keepdims=True), axis=1, keepdims=True)
+    out[BOUND_ROW:, :] = jnp.broadcast_to(largest, (8, 256))
+
+
+def answer_kernel(total, gains, outputs_t, power, csd):
+    packed = total[...]
     r = lax.broadcasted_iota(jnp.int32, (128, 128), 0)
     s = lax.broadcasted_iota(jnp.int32, (128, 128), 1)
     corner = packed[0:128, 0:128]
@@ -230,22 +239,21 @@
 
 
 VMEM = pl.BlockSpec(memory_space=pltpu.VMEM)
-SMEM = pl.BlockSpec(memory_space=pltpu.SMEM)
-
-
-def call(kernel, specs, outs, *operands):
+
+
+def call(kernel, specs, outs, *operands, cost=None):
     return pl.pallas_call(
         kernel,
         in_specs=specs,
         out_specs=[VMEM] * len(outs) if len(outs) > 1 else VMEM,
         out_shape=outs if len(outs) > 1 else outs[0],
+        cost_estimate=cost and pl.CostEstimate(flops=cost, bytes_accessed=0, transcendentals=0),
         compiler_params=pltpu.CompilerParams(vmem_limit_bytes=24 * 2**20),
     )(*operands)
 
 
-def four_chips(packed, first, second, kind):
+def four_chips(sent, first, second):
     core = lax.axis_index("col") & 1
-    sent = packed.astype(kind)
     half = sent.shape[0] // 2
     far = receive(sent, lambda chip, c: (chip ^ (second if c == 0 else first ^ second), c))
     part = lax.dynamic_slice_in_dim(sent, core * half, half, 0)
@@ -257,51 +265,59 @@
         jnp.concatenate([near, near_other], axis=0),
         jnp.concatenate([near_other, near], axis=0),
     )
-    return sent, near_all, far, far_other
+    return near_all, far, far_other
+
+
+def scaled(packed):
+    exponent = jnp.clip(jnp.round(jnp.log2(packed[BOUND_ROW : BOUND_ROW + 1])), -100.0, 100.0)
+    row = lax.broadcasted_iota(jnp.int32, packed.shape, 0)
+    return jnp.where(row < BOUND_ROW, packed * jnp.exp2(-exponent), exponent).astype(jnp.float16)
+
+
+def unscaled(sent):
+    wide = sent.astype(jnp.float32)
+    return wide * jnp.exp2(wide[BOUND_ROW : BOUND_ROW + 1])
+
+
+def pack(mode_shapes, coords):
+    modes = mode_shapes.shape[0]
+    high, low = (coords >> 8).astype(jnp.bfloat16), (coords & 255).astype(jnp.bfloat16)
+    return (
+        jnp.pad(mode_shapes, ((0, POINT_ROWS), (0, 0)))
+        + jnp.pad(high, ((modes, POINT_ROWS - 3), (0, 0)))
+        + jnp.pad(low, ((modes + 8, POINT_ROWS - 11), (0, 0)))
+    )
 
 
 def local_chips(coords, mode_shapes, output_shapes, response_gain):
-    row, col = lax.axis_index("row"), lax.axis_index("col")
-    core = col & 1
-    x, y, z = col >> 1, row & 1, (row >> 1) & 1
-    bits = jnp.stack(
-        [
-            core,
-            jnp.where(core == 0, x, y),
-            jnp.where(core == 0, 1 - y, y),
-            z,
-        ]
-    ).astype(jnp.int32)
-    blank = jnp.zeros((5, coords.shape[1]), jnp.bfloat16)
-    high = (coords >> 8).astype(jnp.bfloat16)
-    low = (coords & 255).astype(jnp.bfloat16)
-    packed = jnp.concatenate([mode_shapes, high, blank, low, blank], axis=0)
+    modes, nodes = mode_shapes.shape
+    packed = pack(mode_shapes, coords)
+    own = jnp.stack([packed, pack(other_core(mode_shapes), other_core(coords))])
     c_own = receive(packed, lambda chip, c: (chip ^ (BIT_W if chip < BIT_W else BIT_W | BIT_Z), c))
-    own = jnp.stack([packed, other_core(packed)])
     a = receive(own, lambda chip, c: (chip ^ (BIT_X if c == 0 else BIT_Y), c))
     b = receive(own, lambda chip, c: (chip ^ (BIT_Z if c == 0 else BIT_X | BIT_Y | BIT_Z), c))
     c_other = other_core(c_own)
     e = other_core(a)
-    modes = mode_shapes.shape[0]
     square = jax.ShapeDtypeStruct((modes, modes), jnp.float32)
     tri = jax.ShapeDtypeStruct((modes // 2 + 16, modes), jnp.float32)
-    early = call(early_kernel, [VMEM] * 5 + [SMEM], [square], own, a, e, c_own, c_other, bits)
-    mine = call(late_kernel, [VMEM] * 6 + [SMEM, VMEM], [tri], own, a, b, e, c_own, c_other, bits, early)
+    gain_rows = jax.ShapeDtypeStruct(response_gain.shape, jnp.float32)
+    early, gains = call(early_kernel, [VMEM] * 6, [square, gain_rows], own, a, e, c_own, c_other, response_gain)
+    mine = call(late_kernel, [VMEM] * 7, [tri], own, a, b, e, c_own, c_other, early)
     chip_sum = mine + other_core(mine)
-    s, pa, pb, pc = four_chips(chip_sum, BIT_Z, BIT_W, jnp.bfloat16)
     f = jnp.float32
-    line_sum = (s.astype(f) + pa.astype(f)) + (pb.astype(f) + pc.astype(f))
-    s, pa, pb, pc = four_chips(line_sum, BIT_X, BIT_Y, jnp.float32)
+    sent = chip_sum.astype(jnp.bfloat16)
+    pa, pb, pc = four_chips(sent, BIT_Z, BIT_W)
+    line_sum = (sent.astype(f) + pa.astype(f)) + (pb.astype(f) + pc.astype(f))
+    sent = scaled(line_sum)
+    pa, pb, pc = four_chips(sent, BIT_X, BIT_Y)
+    total = (unscaled(sent) + unscaled(pa)) + (unscaled(pb) + unscaled(pc))
     count = output_shapes.shape[0]
     power, csd = call(
         answer_kernel,
-        [VMEM] * 6,
+        [VMEM] * 3,
         [jax.ShapeDtypeStruct((1, count), jnp.float32), square],
-        s,
-        pa,
-        pb,
-        pc,
-        response_gain,
+        total,
+        gains,
         output_shapes.T,
     )
     return (power.reshape(count), csd)

time: 39.2 us -> 36.7 us (0.936)
  waiting for transfers between devices: 13.3 us -> 11 us
  local copies, waits for them, and re-layouts: 1.9 us -> 0.67 us
  other arithmetic: 0.86 us -> 1.9 us
  starting transfers between devices: 17.1 us -> 18.1 us
  Pallas kernels: 5.05 us -> 4.1 us
    ppermute x15 -> x16, waiting for transfers between devices: 13.3 us -> 11 us  [receive(): return lax.ppermute(array, axes, pairs)]
    pallas_call x3, Pallas kernels: 5.05 us -> 4.1 us  [call(): pl.pallas_call(kernel, in_specs=specs, out_specs=[VMEM] * len(outs) if le...]
    ppermute x15 -> x16, starting transfers between devices: 17.1 us -> 18.1 us  [receive(): return lax.ppermute(array, axes, pairs)]
    add x1 -> x3, other arithmetic: 0.05 us -> 0.98 us  [the longest x1 0.86 us: pack(): jnp.pad(mode_shapes, ((0, POINT_ROWS), (0, 0)))]
    concatenate x1 -> x0, local copies, waits for them, and re-layouts: 0.91 us -> none  [local_chips(): packed = jnp.concatenate([mode_shapes, high, blank, low, blank], axis=0)]
    convert_element_type x2 -> x7, other arithmetic: 0.7 us -> 0.85 us  [the longest x2 0.69 us: pack(): (coords >> 8).astype(jnp.bfloat16)]
  transfers between devices with their start and end apart: 15 -> 16, of which waited for: 10 -> 8; matrix products, arithmetic and copies ran while one was open for 2% -> 6% of each run, Pallas kernels for 5% -> 4%
where the time goes in v2:
time: 36.7 us; the launch traced here: 36.5 us
  starting transfers between devices  18.1 us (49%)
  waiting for transfers between devices  11 us (30%)
  Pallas kernels  4.1 us (11%)
  other arithmetic  1.9 us (5%)
  between operations  0.78 us (2%)
  local copies, waits for them, and re-layouts  0.67 us (2%)
    ppermute x16, starting transfers between devices, receive(): return lax.ppermute(array, axes, pairs)  18.1 us
    ppermute x16, waiting for transfers between devices, receive(): return lax.ppermute(array, axes, pairs)  11 us
    pallas_call x3, Pallas kernels, call(): pl.pallas_call(kernel, in_specs=specs, out_specs=[VMEM] * len(outs) if le...  4.1 us
    add x1, other arithmetic, pack(): jnp.pad(mode_shapes, ((0, POINT_ROWS), (0, 0)))  0.86 us
  transfers between devices with their start and end apart: 16, of which 8 were waited for; matrix products, arithmetic and copies ran while one was open for 6% of the time, Pallas kernels for 4%

profile of v2, /device:TPU:0, one launch (start us, length us, event | category | flops | bytes accessed | tf_op | source)
XLA Modules:
  0.0 36.5 jit_solution(10639654365807642135)
XLA Ops:
  0.6 0.5 %collective-permute-start.1 = (s32[3,128]{1,0:T(4,128)}, s32[3,128]{1,0:T(4,128)S(1)}, u32[]{:S(2)}, u32[]{:S(2)}) collective-permute-start(s32[3,128]{1,0:T(4,128)} %param.4), channel_id=1, source_target_pairs={{1,0},{0,1},{3,2},{2,3},{5,4},{4,5},{7,6},{6,7},{9,8},{8,9},{11,10... | collective-permute-start | bytes 4616 | tf_op jit(solution)/shard_map/ppermute | solution.py:83
  1.2 0.7 %shift-right-arithmetic_convert_fusion.1 = (bf16[3,128]{1,0:T(4,128)(2,1)S(1)}, bf16[3,128]{1,0:T(4,128)(2,1)S(1)}) fusion(s32[3,128]{1,0:T(4,128)} %param.4), kind=kLoop, calls=%fused_computation.13 | loop fusion | flops 1536 | bytes 3072 | tf_op jit(solution)/shard_map/convert_element_type | solution.py:284
  1.9 0.9 %pad_add_fusion = (bf16[272,128]{1,0:T(8,128)(2,1)S(1)}, bf16[1,272,128]{2,1,0:T(8,128)(2,1)S(1)}) fusion(bf16[3,128]{1,0:T(4,128)(2,1)S(1)} %get-tuple-element.17, bf16[3,128]{1,0:T(4,128)(2,1)S(1)} %get-tuple-element.16, bf16[256,128]{1,0:T(8,128)(2,1)} %param.5), kind=kLoop, calls=%fused_computation.9 | loop fusion | flops 208896 | bytes 206336 | tf_op jit(solution)/shard_map/add | solution.py:286
  2.9 3.0 %collective-permute-start.2 = (bf16[2,272,128]{2,1,0:T(8,128)(2,1)S(1)}, bf16[2,272,128]{2,1,0:T(8,128)(2,1)S(1)}, u32[]{:S(2)}, u32[]{:S(2)}) collective-permute-start(bf16[2,272,128]{2,1,0:T(8,128)(2,1)S(1)} %pad_maximum_fusion.own), channel_id=1, source_target_pairs={{2,0},{5,1},{0,2},{7,3},{6,4},{1,5},{4,6},{3,7},{10,8},{13,9},{8,1... | collective-permute-start | bytes 417800 | tf_op jit(solution)/shard_map/ppermute | solution.py:83
  5.8 3.6 %collective-permute-start.5 = (bf16[272,128]{1,0:T(8,128)(2,1)S(1)}, bf16[272,128]{1,0:T(8,128)(2,1)S(1)}, u32[]{:S(2)}, u32[]{:S(2)}) collective-permute-start(bf16[272,128]{1,0:T(8,128)(2,1)S(1)} %get-tuple-element.14), channel_id=1, source_target_pairs={{16,0},{17,1},{18,2},{19,3},{20,4},{21,5},{22,6},{23,7},{24,8},{25... | collective-permute-start | bytes 208904 | tf_op jit(solution)/shard_map/ppermute | solution.py:83
  9.5 1.5 %collective-permute-start.3 = (bf16[2,272,128]{2,1,0:T(8,128)(2,1)S(1)}, bf16[2,272,128]{2,1,0:T(8,128)(2,1)S(1)}, u32[]{:S(2)}, u32[]{:S(2)}) collective-permute-start(bf16[2,272,128]{2,1,0:T(8,128)(2,1)S(1)} %pad_maximum_fusion.own), channel_id=1, source_target_pairs={{8,0},{15,1},{10,2},{13,3},{12,4},{11,5},{14,6},{9,7},{0,8},{7,9},... | collective-permute-start | bytes 417800 | tf_op jit(solution)/shard_map/ppermute | solution.py:83
  11.0 1.4 %collective-permute-done.5.c_own = bf16[272,128]{1,0:T(8,128)(2,1)S(1)} collective-permute-done((bf16[272,128]{1,0:T(8,128)(2,1)S(1)}, bf16[272,128]{1,0:T(8,128)(2,1)S(1)}, u32[]{:S(2)}, u32[]{:S(2)}) %collective-permute-start.5) | collective-permute-done | bytes 69664 | tf_op jit(solution)/shard_map/ppermute | solution.py:83
  12.4 0.7 %collective-permute-start.6 = (bf16[272,128]{1,0:T(8,128)(2,1)S(1)}, bf16[272,128]{1,0:T(8,128)(2,1)S(1)}, u32[]{:S(2)}, u32[]{:S(2)}) collective-permute-start(bf16[272,128]{1,0:T(8,128)(2,1)S(1)} %collective-permute-done.5.c_own), channel_id=1, source_target_pairs={{1,0},{0,1},{3,2},{2,3},{5,4},{4,5},{7,6},{6,7},{9,8},{8,9},{11,10... | collective-permute-start | bytes 208904 | tf_op jit(solution)/shard_map/ppermute | solution.py:83
  13.1 0.9 %collective-permute-done.6.c_other = bf16[272,128]{1,0:T(8,128)(2,1)S(1)} collective-permute-done((bf16[272,128]{1,0:T(8,128)(2,1)S(1)}, bf16[272,128]{1,0:T(8,128)(2,1)S(1)}, u32[]{:S(2)}, u32[]{:S(2)}) %collective-permute-start.6) | collective-permute-done | bytes 69664 | tf_op jit(solution)/shard_map/ppermute | solution.py:83
  14.0 1.4 %shard_map.59 = (f32[256,256]{1,0:T(8,128)S(1)}, f32[2,256]{1,0:T(2,128)S(1)}) custom-call(bf16[2,272,128]{2,1,0:T(8,128)(2,1)S(1)} %pad_maximum_fusion.own, bf16[2,272,128]{2,1,0:T(8,128)(2,1)S(1)} %collective-permute-done.2.a, bf16[2,272,128]{2,1,0:T(8,128)(2,1)S(1)} %collective-permute-done.4.e, bf16[272,128]{1,0:T(8,128)(2,1)S(1)} %collective-permute-done.5.c_own, ...), custom_call_target="tpu_custom_call" | custom-call | tf_op jit(solution)/shard_map/pallas_call | solution.py:245
  15.5 1.4 %shard_map.60 = f32[144,256]{1,0:T(8,128)S(1)} custom-call(bf16[2,272,128]{2,1,0:T(8,128)(2,1)S(1)} %pad_maximum_fusion.own, bf16[2,272,128]{2,1,0:T(8,128)(2,1)S(1)} %collective-permute-done.2.a, bf16[2,272,128]{2,1,0:T(8,128)(2,1)S(1)} %collective-permute-done.3.b, bf16[2,272,128]{2,1,0:T(8,128)(2,1)S(1)} %collective-permute-done.4.e, ...), custom_call_target="tpu_custom_call" | custom-call | tf_op jit(solution)/shard_map/pallas_call | solution.py:245
  16.9 1.3 %collective-permute-start.7 = (f32[144,256]{1,0:T(8,128)S(1)}, f32[144,256]{1,0:T(8,128)S(1)}, u32[]{:S(2)}, u32[]{:S(2)}) collective-permute-start(f32[144,256]{1,0:T(8,128)S(1)} %shard_map.60), channel_id=1, source_target_pairs={{1,0},{0,1},{3,2},{2,3},{5,4},{4,5},{7,6},{6,7},{9,8},{8,9},{11,10... | collective-permute-start | bytes 442376 | tf_op jit(solution)/shard_map/ppermute | solution.py:83
  18.1 1.0 %collective-permute-done.7 = f32[144,256]{1,0:T(8,128)S(1)} collective-permute-done((f32[144,256]{1,0:T(8,128)S(1)}, f32[144,256]{1,0:T(8,128)S(1)}, u32[]{:S(2)}, u32[]{:S(2)}) %collective-permute-start.7) | collective-permute-done | bytes 147488 | tf_op jit(solution)/shard_map/ppermute | solution.py:83
  19.1 2.6 %collective-permute-start.10 = (bf16[144,256]{1,0:T(8,128)(2,1)S(1)}, bf16[144,256]{1,0:T(8,128)(2,1)S(1)}, u32[]{:S(2)}, u32[]{:S(2)}) collective-permute-start(bf16[144,256]{1,0:T(8,128)(2,1)S(1)} %add_convert_fusion), channel_id=1, source_target_pairs={{16,0},{25,1},{18,2},{27,3},{20,4},{29,5},{22,6},{31,7},{24,8},{17... | collective-permute-start | bytes 221192 | tf_op jit(solution)/shard_map/ppermute | solution.py:83
  21.7 1.6 %collective-permute-start.8 = (bf16[72,256]{1,0:T(8,128)(2,1)S(1)}, bf16[72,256]{1,0:T(8,128)(2,1)S(1)}, u32[]{:S(2)}, u32[]{:S(2)}) collective-permute-start(bf16[72,256]{1,0:T(8,128)(2,1)S(1)} %constant_dynamic-slice_fusion.1), channel_id=1, source_target_pairs={{8,0},{9,1},{10,2},{11,3},{12,4},{13,5},{14,6},{15,7},{0,8},{1,9},... | collective-permute-start | bytes 110600 | tf_op jit(solution)/shard_map/ppermute | solution.py:83
  23.3 3.2 %collective-permute-done.8 = bf16[72,256]{1,0:T(8,128)(2,1)S(1)} collective-permute-done((bf16[72,256]{1,0:T(8,128)(2,1)S(1)}, bf16[72,256]{1,0:T(8,128)(2,1)S(1)}, u32[]{:S(2)}, u32[]{:S(2)}) %collective-permute-start.8) | collective-permute-done | bytes 36896 | tf_op jit(solution)/shard_map/ppermute | solution.py:83
  26.6 0.4 %collective-permute-start.11 = (bf16[144,256]{1,0:T(8,128)(2,1)S(1)}, bf16[144,256]{1,0:T(8,128)(2,1)S(1)}, u32[]{:S(2)}, u32[]{:S(2)}) collective-permute-start(bf16[144,256]{1,0:T(8,128)(2,1)S(1)} %collective-permute-done.10), channel_id=1, source_target_pairs={{1,0},{0,1},{3,2},{2,3},{5,4},{4,5},{7,6},{6,7},{9,8},{8,9},{11,10... | collective-permute-start | bytes 221192 | tf_op jit(solution)/shard_map/ppermute | solution.py:83
  27.0 0.6 %copy.6 = bf16[2048,256]{0,1:T(8,128)(2,1)S(1)} copy(bf16[2048,256]{1,0:T(8,128)(2,1)S(1)} %copy-done.1) | data formatting | bytes 2097152 | tf_op args[2]
  28.1 1.5 %collective-permute-start.14 = (f16[144,256]{1,0:T(8,128)(2,1)S(1)}, f16[144,256]{1,0:T(8,128)(2,1)S(1)}, u32[]{:S(2)}, u32[]{:S(2)}) collective-permute-start(f16[144,256]{1,0:T(8,128)(2,1)S(1)} %get-tuple-element.11), channel_id=1, source_target_pairs={{4,0},{7,1},{6,2},{5,3},{0,4},{3,5},{2,6},{1,7},{12,8},{15,9},{14,... | collective-permute-start | bytes 221192 | tf_op jit(solution)/shard_map/ppermute | solution.py:83
  29.7 0.7 %collective-permute-start.12 = (f16[72,256]{1,0:T(8,128)(2,1)S(1)}, f16[72,256]{1,0:T(8,128)(2,1)S(1)}, u32[]{:S(2)}, u32[]{:S(2)}) collective-permute-start(f16[72,256]{1,0:T(8,128)(2,1)S(1)} %constant_dynamic-slice_fusion), channel_id=1, source_target_pairs={{2,0},{3,1},{0,2},{1,3},{6,4},{7,5},{4,6},{5,7},{10,8},{11,9},{8,1... | collective-permute-start | bytes 110600 | tf_op jit(solution)/shard_map/ppermute | solution.py:83
  30.4 3.3 %collective-permute-done.12 = f16[72,256]{1,0:T(8,128)(2,1)S(1)} collective-permute-done((f16[72,256]{1,0:T(8,128)(2,1)S(1)}, f16[72,256]{1,0:T(8,128)(2,1)S(1)}, u32[]{:S(2)}, u32[]{:S(2)}) %collective-permute-start.12) | collective-permute-done | bytes 36896 | tf_op jit(solution)/shard_map/ppermute | solution.py:83
  33.7 0.6 %collective-permute-start.15 = (f16[144,256]{1,0:T(8,128)(2,1)S(1)}, f16[144,256]{1,0:T(8,128)(2,1)S(1)}, u32[]{:S(2)}, u32[]{:S(2)}) collective-permute-start(f16[144,256]{1,0:T(8,128)(2,1)S(1)} %collective-permute-done.14), channel_id=1, source_target_pairs={{1,0},{0,1},{3,2},{2,3},{5,4},{4,5},{7,6},{6,7},{9,8},{8,9},{11,10... | collective-permute-start | bytes 221192 | tf_op jit(solution)/shard_map/ppermute | solution.py:83
  34.2 0.6 %collective-permute-done.13 = f16[72,256]{1,0:T(8,128)(2,1)S(1)} collective-permute-done((f16[72,256]{1,0:T(8,128)(2,1)S(1)}, f16[72,256]{1,0:T(8,128)(2,1)S(1)}, u32[]{:S(2)}, u32[]{:S(2)}) %collective-permute-start.13) | collective-permute-done | bytes 36896 | tf_op jit(solution)/shard_map/ppermute | solution.py:83
  35.3 1.3 %shard_map.61 = (f32[1,2048]{1,0:T(1,128)}, f32[256,256]{1,0:T(8,128)}) custom-call(f32[144,256]{1,0:T(8,128)S(1)} %add_add_fusion.total, f32[2,256]{1,0:T(2,128)S(1)} %get-tuple-element.7.gains, bf16[256,2048]{1,0:T(8,128)(2,1)S(1)} %bitcast.12), custom_call_target="tpu_custom_call" | custom-call | tf_op jit(solution)/shard_map/pallas_call | solution.py:245
  (36 shorter events, 1.1 us)
Async XLA Ops:
  0.6 2.1 %collective-permute-start.1 = (s32[3,128]{1,0:T(4,128)}, s32[3,128]{1,0:T(4,128)S(1)}, u32[]{:S(2)}, u32[]{:S(2)}) collective-permute-start(s32[3,128]{1,0:T(4,128)} %param.4), channel_id=1, source_target_pairs={{1,0},{0,1},{3,2},{2,3},{5,4},{4,5},{7,6},{6,7},{9,8},{8,9},{11,10... | collective-permute-start | bytes 4616 | tf_op jit(solution)/shard_map/ppermute | solution.py:83
  1.1 1.7 %collective-permute-start = (bf16[256,128]{1,0:T(8,128)(2,1)}, bf16[256,128]{1,0:T(8,128)(2,1)S(1)}, u32[]{:S(2)}, u32[]{:S(2)}) collective-permute-start(bf16[256,128]{1,0:T(8,128)(2,1)} %param.5), channel_id=1, source_target_pairs={{1,0},{0,1},{3,2},{2,3},{5,4},{4,5},{7,6},{6,7},{9,8},{8,9},{11,10... | collective-permute-start | bytes 196616 | tf_op jit(solution)/shard_map/ppermute | solution.py:83
  2.8 11.2 %copy-start = (f32[2,256]{1,0:T(2,128)S(1)}, f32[2,256]{1,0:T(2,128)}, u32[]{:S(2)}) copy-start(f32[2,256]{1,0:T(2,128)} %response_gain.1) | copy-start | bytes 6148
  2.9 6.6 %collective-permute-start.2 = (bf16[2,272,128]{2,1,0:T(8,128)(2,1)S(1)}, bf16[2,272,128]{2,1,0:T(8,128)(2,1)S(1)}, u32[]{:S(2)}, u32[]{:S(2)}) collective-permute-start(bf16[2,272,128]{2,1,0:T(8,128)(2,1)S(1)} %pad_maximum_fusion.own), channel_id=1, source_target_pairs={{2,0},{5,1},{0,2},{7,3},{6,4},{1,5},{4,6},{3,7},{10,8},{13,9},{8,1... | collective-permute-start | bytes 417800 | tf_op jit(solution)/shard_map/ppermute | solution.py:83
  5.8 21.2 %copy-start.1 = (bf16[2048,256]{1,0:T(8,128)(2,1)S(1)}, bf16[2048,256]{1,0:T(8,128)(2,1)}, u32[]{:S(2)}) copy-start(bf16[2048,256]{1,0:T(8,128)(2,1)} %param.6) | copy-start | bytes 3145732
  5.8 6.6 %collective-permute-start.5 = (bf16[272,128]{1,0:T(8,128)(2,1)S(1)}, bf16[272,128]{1,0:T(8,128)(2,1)S(1)}, u32[]{:S(2)}, u32[]{:S(2)}) collective-permute-start(bf16[272,128]{1,0:T(8,128)(2,1)S(1)} %get-tuple-element.14), channel_id=1, source_target_pairs={{16,0},{17,1},{18,2},{19,3},{20,4},{21,5},{22,6},{23,7},{24,8},{25... | collective-permute-start | bytes 208904 | tf_op jit(solution)/shard_map/ppermute | solution.py:83
  9.4 4.6 %collective-permute-start.4 = (bf16[2,272,128]{2,1,0:T(8,128)(2,1)S(1)}, bf16[2,272,128]{2,1,0:T(8,128)(2,1)S(1)}, u32[]{:S(2)}, u32[]{:S(2)}) collective-permute-start(bf16[2,272,128]{2,1,0:T(8,128)(2,1)S(1)} %collective-permute-done.2.a), channel_id=1, source_target_pairs={{1,0},{0,1},{3,2},{2,3},{5,4},{4,5},{7,6},{6,7},{9,8},{8,9},{11,10... | collective-permute-start | bytes 417800 | tf_op jit(solution)/shard_map/ppermute | solution.py:83
  9.5 6.0 %collective-permute-start.3 = (bf16[2,272,128]{2,1,0:T(8,128)(2,1)S(1)}, bf16[2,272,128]{2,1,0:T(8,128)(2,1)S(1)}, u32[]{:S(2)}, u32[]{:S(2)}) collective-permute-start(bf16[2,272,128]{2,1,0:T(8,128)(2,1)S(1)} %pad_maximum_fusion.own), channel_id=1, source_target_pairs={{8,0},{15,1},{10,2},{13,3},{12,4},{11,5},{14,6},{9,7},{0,8},{7,9},... | collective-permute-start | bytes 417800 | tf_op jit(solution)/shard_map/ppermute | solution.py:83
  12.4 1.6 %collective-permute-start.6 = (bf16[272,128]{1,0:T(8,128)(2,1)S(1)}, bf16[272,128]{1,0:T(8,128)(2,1)S(1)}, u32[]{:S(2)}, u32[]{:S(2)}) collective-permute-start(bf16[272,128]{1,0:T(8,128)(2,1)S(1)} %collective-permute-done.5.c_own), channel_id=1, source_target_pairs={{1,0},{0,1},{3,2},{2,3},{5,4},{4,5},{7,6},{6,7},{9,8},{8,9},{11,10... | collective-permute-start | bytes 208904 | tf_op jit(solution)/shard_map/ppermute | solution.py:83
  16.9 2.3 %collective-permute-start.7 = (f32[144,256]{1,0:T(8,128)S(1)}, f32[144,256]{1,0:T(8,128)S(1)}, u32[]{:S(2)}, u32[]{:S(2)}) collective-permute-start(f32[144,256]{1,0:T(8,128)S(1)} %shard_map.60), channel_id=1, source_target_pairs={{1,0},{0,1},{3,2},{2,3},{5,4},{4,5},{7,6},{6,7},{9,8},{8,9},{11,10... | collective-permute-start | bytes 442376 | tf_op jit(solution)/shard_map/ppermute | solution.py:83
  19.1 7.5 %collective-permute-start.10 = (bf16[144,256]{1,0:T(8,128)(2,1)S(1)}, bf16[144,256]{1,0:T(8,128)(2,1)S(1)}, u32[]{:S(2)}, u32[]{:S(2)}) collective-permute-start(bf16[144,256]{1,0:T(8,128)(2,1)S(1)} %add_convert_fusion), channel_id=1, source_target_pairs={{16,0},{25,1},{18,2},{27,3},{20,4},{29,5},{22,6},{31,7},{24,8},{17... | collective-permute-start | bytes 221192 | tf_op jit(solution)/shard_map/ppermute | solution.py:83
  21.7 4.8 %collective-permute-start.8 = (bf16[72,256]{1,0:T(8,128)(2,1)S(1)}, bf16[72,256]{1,0:T(8,128)(2,1)S(1)}, u32[]{:S(2)}, u32[]{:S(2)}) collective-permute-start(bf16[72,256]{1,0:T(8,128)(2,1)S(1)} %constant_dynamic-slice_fusion.1), channel_id=1, source_target_pairs={{8,0},{9,1},{10,2},{11,3},{12,4},{13,5},{14,6},{15,7},{0,8},{1,9},... | collective-permute-start | bytes 110600 | tf_op jit(solution)/shard_map/ppermute | solution.py:83
  26.5 1.2 %collective-permute-start.9 = (bf16[72,256]{1,0:T(8,128)(2,1)S(1)}, bf16[72,256]{1,0:T(8,128)(2,1)S(1)}, u32[]{:S(2)}, u32[]{:S(2)}) collective-permute-start(bf16[72,256]{1,0:T(8,128)(2,1)S(1)} %collective-permute-done.8), channel_id=1, source_target_pairs={{1,0},{0,1},{3,2},{2,3},{5,4},{4,5},{7,6},{6,7},{9,8},{8,9},{11,10... | collective-permute-start | bytes 110600 | tf_op jit(solution)/shard_map/ppermute | solution.py:83
  26.6 1.3 %collective-permute-start.11 = (bf16[144,256]{1,0:T(8,128)(2,1)S(1)}, bf16[144,256]{1,0:T(8,128)(2,1)S(1)}, u32[]{:S(2)}, u32[]{:S(2)}) collective-permute-start(bf16[144,256]{1,0:T(8,128)(2,1)S(1)} %collective-permute-done.10), channel_id=1, source_target_pairs={{1,0},{0,1},{3,2},{2,3},{5,4},{4,5},{7,6},{6,7},{9,8},{8,9},{11,10... | collective-permute-start | bytes 221192 | tf_op jit(solution)/shard_map/ppermute | solution.py:83
  28.1 5.5 %collective-permute-start.14 = (f16[144,256]{1,0:T(8,128)(2,1)S(1)}, f16[144,256]{1,0:T(8,128)(2,1)S(1)}, u32[]{:S(2)}, u32[]{:S(2)}) collective-permute-start(f16[144,256]{1,0:T(8,128)(2,1)S(1)} %get-tuple-element.11), channel_id=1, source_target_pairs={{4,0},{7,1},{6,2},{5,3},{0,4},{3,5},{2,6},{1,7},{12,8},{15,9},{14,... | collective-permute-start | bytes 221192 | tf_op jit(solution)/shard_map/ppermute | solution.py:83
  29.7 4.0 %collective-permute-start.12 = (f16[72,256]{1,0:T(8,128)(2,1)S(1)}, f16[72,256]{1,0:T(8,128)(2,1)S(1)}, u32[]{:S(2)}, u32[]{:S(2)}) collective-permute-start(f16[72,256]{1,0:T(8,128)(2,1)S(1)} %constant_dynamic-slice_fusion), channel_id=1, source_target_pairs={{2,0},{3,1},{0,2},{1,3},{6,4},{7,5},{4,6},{5,7},{10,8},{11,9},{8,1... | collective-permute-start | bytes 110600 | tf_op jit(solution)/shard_map/ppermute | solution.py:83
  33.6 1.2 %collective-permute-start.13 = (f16[72,256]{1,0:T(8,128)(2,1)S(1)}, f16[72,256]{1,0:T(8,128)(2,1)S(1)}, u32[]{:S(2)}, u32[]{:S(2)}) collective-permute-start(f16[72,256]{1,0:T(8,128)(2,1)S(1)} %collective-permute-done.12), channel_id=1, source_target_pairs={{1,0},{0,1},{3,2},{2,3},{5,4},{4,5},{7,6},{6,7},{9,8},{8,9},{11,10... | collective-permute-start | bytes 110600 | tf_op jit(solution)/shard_map/ppermute | solution.py:83
  33.7 1.5 %collective-permute-start.15 = (f16[144,256]{1,0:T(8,128)(2,1)S(1)}, f16[144,256]{1,0:T(8,128)(2,1)S(1)}, u32[]{:S(2)}, u32[]{:S(2)}) collective-permute-start(f16[144,256]{1,0:T(8,128)(2,1)S(1)} %collective-permute-done.14), channel_id=1, source_target_pairs={{1,0},{0,1},{3,2},{2,3},{5,4},{4,5},{7,6},{6,7},{9,8},{8,9},{11,10... | collective-permute-start | bytes 221192 | tf_op jit(solution)/shard_map/ppermute | solution.py:83

commit v3 on v2

--- a/solution.py
+++ b/solution.py
@@ -1,4 +1,3 @@
-import functools
 import math
 
 import jax
@@ -20,7 +19,7 @@
 period_shift = 1.5 * 2.0**24
 axes = ("row", "col")
 POINT_ROWS = 16
-BOUND_ROW = 136
+BOUND_ROW = 132
 
 
 def coherence(left_points, right_points):
@@ -72,6 +71,9 @@
 
 
 BIT_X, BIT_Y, BIT_Z, BIT_W = 1, 2, 4, 8
+OFFSET_A = (4, 6)
+OFFSET_B = (1, 3)
+OFFSET_C = (8, 12)
 
 
 def receive(array, source):
@@ -155,64 +157,46 @@
     return dot_t(beside(*projections), beside(*shapes))
 
 
-def place():
+def upper_bits(*roles):
     row, col = lax.axis_index("row"), lax.axis_index("col")
-    return col & 1, col >> 1, row & 1, (row >> 1) & 1
+    core, chip = col & 1, row * 2 + (col >> 1)
+    found = []
+    for left_0, left_1, right_0, right_1 in roles:
+        shift_0, shift_1 = ((d & -d).bit_length() - 1 for d in (left_0 ^ right_0, left_1 ^ right_1))
+        on_0, on_1 = ((chip ^ left_0) >> shift_0) & 1, ((chip ^ left_1) >> shift_1) & 1
+        found.append(jnp.where(core == 0, on_0, on_1))
+    return found
+
+
+ROLE_S, ROLE_A, ROLE_B, ROLE_E = (0, 0), OFFSET_A, OFFSET_B, OFFSET_A[::-1]
 
 
 def early_kernel(own, a, e, c_own, c_other, response_gain, out, gains):
     gains[...] = response_gain[...]
-    core, x, y, _ = place()
-    mine = right_points(own[0])
-    total = 0.5 * dot_t(
-        dot(
-            beside(shapes_of(own[0]), shapes_of(own[1])),
-            jnp.concatenate(
-                [coherence_tile(left_points(own[0]), mine), coherence_tile(left_points(own[1]), mine)], axis=0
-            ),
-        ).astype(jnp.bfloat16),
-        shapes_of(own[0]),
-    )
-    u = jnp.where(core == 0, x, y)
-    jobs = []
-    for k in range(2):
-        left_half, right_half = u * k, u | k
-        jobs.append(quarter(own[left_half ^ core], a[right_half ^ core]))
-    total += paired(jobs)
-    u = jnp.where(core == 0, 1 - y, y)
-    left_half = jnp.where(u == 1, 1, core)
-    right_half = jnp.where(u == 1, core, 0)
-    projection, shapes = quarter(e[left_half ^ (1 - core)], a[right_half ^ core])
-    total += dot_t(projection, shapes)
+    sa, ea = upper_bits(ROLE_S + ROLE_A, ROLE_E + ROLE_A)
+    total = paired([quarter(own[0], a[1]), quarter(own[sa], a[sa]), quarter(e[...], a[ea])])
     total += full_pair([a[0], a[1]], [c_own[...], c_other[...]])
+    total += 0.5 * full_pair([own[0], own[1]], [own[0]])
     out[...] = total
 
 
 def late_kernel(own, a, b, e, c_own, c_other, early, out):
-    core, _, _, u = place()
+    sb, ab, eb = upper_bits(ROLE_S + ROLE_B, ROLE_A + ROLE_B, ROLE_E + ROLE_B)
     total = early[...]
-    jobs = []
-    for k in range(2):
-        left_half, right_half = u * k, u | k
-        jobs.append(quarter(own[left_half ^ core], b[right_half ^ core]))
-    total += paired(jobs)
-    left_half = jnp.where(u == 1, 1, core)
-    right_half = jnp.where(u == 1, core, 0)
-    right = b[right_half ^ core]
-    total += paired([quarter(a[left_half ^ core], right), quarter(e[left_half ^ (1 - core)], right)])
     total += full_pair([b[0], b[1]], [c_own[...], c_other[...]])
+    total += paired([quarter(own[0], b[1]), quarter(own[sb], b[sb]), quarter(a[0], b[ab]), quarter(e[...], b[eb])])
     first = total[0:128, 0:128] + total[0:128, 0:128].T
     second = total[128:256, 128:256] + total[128:256, 128:256].T
     cross = total[0:128, 128:256] + total[128:256, 0:128].T
     r = lax.broadcasted_iota(jnp.int32, (128, 128), 0)
     s = lax.broadcasted_iota(jnp.int32, (128, 128), 1)
-    out[0:128, 0:128] = jnp.where(r <= s, first, second)
+    corner = jnp.where(r <= s, first, second)
+    out[0:128, 0:128] = corner
     out[0:128, 128:256] = cross
     diagonal = jnp.sum(jnp.where(r == s, second, 0.0), axis=0, keepdims=True)
-    out[128:BOUND_ROW, :] = jnp.broadcast_to(beside(diagonal, diagonal), (8, 256))
-    largest = jnp.maximum(jnp.abs(out[0:128, :]), jnp.abs(out[128:129, :]))
-    largest = jnp.max(jnp.max(largest, axis=0, keepdims=True), axis=1, keepdims=True)
-    out[BOUND_ROW:, :] = jnp.broadcast_to(largest, (8, 256))
+    out[128:BOUND_ROW, :] = jnp.broadcast_to(beside(diagonal, diagonal), (4, 256))
+    largest = jnp.maximum(jnp.max(jnp.abs(beside(corner, cross)), axis=0, keepdims=True), jnp.abs(beside(diagonal, diagonal)))
+    out[BOUND_ROW:, :] = jnp.broadcast_to(largest, (out.shape[0] - BOUND_ROW, 256))
 
 
 def answer_kernel(total, gains, outputs_t, power, csd):
@@ -241,29 +225,29 @@
 VMEM = pl.BlockSpec(memory_space=pltpu.VMEM)
 
 
-def call(kernel, specs, outs, *operands, cost=None):
+def call(kernel, specs, outs, *operands):
     return pl.pallas_call(
         kernel,
         in_specs=specs,
         out_specs=[VMEM] * len(outs) if len(outs) > 1 else VMEM,
         out_shape=outs if len(outs) > 1 else outs[0],
-        cost_estimate=cost and pl.CostEstimate(flops=cost, bytes_accessed=0, transcendentals=0),
         compiler_params=pltpu.CompilerParams(vmem_limit_bytes=24 * 2**20),
     )(*operands)
 
 
 def four_chips(sent, first, second):
     core = lax.axis_index("col") & 1
-    half = sent.shape[0] // 2
+    half = 72
+    rest = sent.shape[0] - half
     far = receive(sent, lambda chip, c: (chip ^ (second if c == 0 else first ^ second), c))
-    part = lax.dynamic_slice_in_dim(sent, core * half, half, 0)
+    part = lax.dynamic_slice_in_dim(sent, core * rest, half, 0)
     near = receive(part, lambda chip, c: (chip ^ first, c))
     far_other = other_core(far)
     near_other = other_core(near)
     near_all = jnp.where(
         core == 0,
-        jnp.concatenate([near, near_other], axis=0),
-        jnp.concatenate([near_other, near], axis=0),
+        jnp.concatenate([near[:rest], near_other], axis=0),
+        jnp.concatenate([near_other[:rest], near], axis=0),
     )
     return near_all, far, far_other
 
@@ -293,13 +277,13 @@
     modes, nodes = mode_shapes.shape
     packed = pack(mode_shapes, coords)
     own = jnp.stack([packed, pack(other_core(mode_shapes), other_core(coords))])
-    c_own = receive(packed, lambda chip, c: (chip ^ (BIT_W if chip < BIT_W else BIT_W | BIT_Z), c))
-    a = receive(own, lambda chip, c: (chip ^ (BIT_X if c == 0 else BIT_Y), c))
-    b = receive(own, lambda chip, c: (chip ^ (BIT_Z if c == 0 else BIT_X | BIT_Y | BIT_Z), c))
+    c_own = receive(packed, lambda chip, c: (chip ^ OFFSET_C[0 if chip < BIT_W else 1], c))
+    a = receive(own, lambda chip, c: (chip ^ OFFSET_A[c], c))
+    b = receive(own, lambda chip, c: (chip ^ OFFSET_B[c], c))
     c_other = other_core(c_own)
-    e = other_core(a)
+    e = other_core(a[1])
     square = jax.ShapeDtypeStruct((modes, modes), jnp.float32)
-    tri = jax.ShapeDtypeStruct((modes // 2 + 16, modes), jnp.float32)
+    tri = jax.ShapeDtypeStruct((modes // 2 + 8, modes), jnp.float32)
     gain_rows = jax.ShapeDtypeStruct(response_gain.shape, jnp.float32)
     early, gains = call(early_kernel, [VMEM] * 6, [square, gain_rows], own, a, e, c_own, c_other, response_gain)
     mine = call(late_kernel, [VMEM] * 7, [tri], own, a, b, e, c_own, c_other, early)

time: 36.7 us -> 34.8 us (0.948)
  waiting for transfers between devices: 11 us -> 9.75 us
  starting transfers between devices: 18.1 us -> 17.6 us
    ppermute x16, waiting for transfers between devices: 11 us -> 9.75 us  [receive(): return lax.ppermute(array, axes, pairs)]
    ppermute x16, starting transfers between devices: 18.1 us -> 17.6 us  [receive(): return lax.ppermute(array, axes, pairs)]
  transfers between devices with their start and end apart: 16 -> 16, of which waited for: 8 -> 10; matrix products, arithmetic and copies ran while one was open for 6% -> 7% of each run, Pallas kernels for 4% -> 4%
where the time goes in v3:
time: 34.8 us; the launch traced here: 34.6 us
  starting transfers between devices  17.6 us (51%)
  waiting for transfers between devices  9.75 us (28%)
  Pallas kernels  3.92 us (11%)
  other arithmetic  1.91 us (5%)
  between operations  0.79 us (2%)
  local copies, waits for them, and re-layouts  0.7 us (2%)
    ppermute x16, starting transfers between devices, receive(): return lax.ppermute(array, axes, pairs)  17.6 us
    ppermute x16, waiting for transfers between devices, receive(): return lax.ppermute(array, axes, pairs)  9.75 us
    pallas_call x3, Pallas kernels, call(): pl.pallas_call(kernel, in_specs=specs, out_specs=[VMEM] * len(outs) if le...  3.92 us
    add x1, other arithmetic, pack(): jnp.pad(mode_shapes, ((0, POINT_ROWS), (0, 0)))  0.86 us
  transfers between devices with their start and end apart: 16, of which 10 were waited for; matrix products, arithmetic and copies ran while one was open for 7% of the time, Pallas kernels for 4%

profile of v3, /device:TPU:0, one launch (start us, length us, event | category | flops | bytes accessed | tf_op | source)
XLA Modules:
  0.0 34.6 jit_solution(10919634115564528499)
XLA Ops:
  0.6 0.5 %collective-permute-start.1 = (s32[3,128]{1,0:T(4,128)}, s32[3,128]{1,0:T(4,128)S(1)}, u32[]{:S(2)}, u32[]{:S(2)}) collective-permute-start(s32[3,128]{1,0:T(4,128)} %param.4), channel_id=1, source_target_pairs={{1,0},{0,1},{3,2},{2,3},{5,4},{4,5},{7,6},{6,7},{9,8},{8,9},{11,10... | collective-permute-start | bytes 4616 | tf_op jit(solution)/shard_map/ppermute | solution.py:85
  1.2 0.7 %shift-right-arithmetic_convert_fusion.1 = (bf16[3,128]{1,0:T(4,128)(2,1)S(1)}, bf16[3,128]{1,0:T(4,128)(2,1)S(1)}) fusion(s32[3,128]{1,0:T(4,128)} %param.4), kind=kLoop, calls=%fused_computation.14 | loop fusion | flops 1536 | bytes 3072 | tf_op jit(solution)/shard_map/convert_element_type | solution.py:268
  1.9 0.9 %pad_add_fusion = (bf16[272,128]{1,0:T(8,128)(2,1)S(1)}, bf16[1,272,128]{2,1,0:T(8,128)(2,1)S(1)}) fusion(bf16[3,128]{1,0:T(4,128)(2,1)S(1)} %get-tuple-element.17, bf16[3,128]{1,0:T(4,128)(2,1)S(1)} %get-tuple-element.16, bf16[256,128]{1,0:T(8,128)(2,1)} %param.5), kind=kLoop, calls=%fused_computation.10 | loop fusion | flops 208896 | bytes 206336 | tf_op jit(solution)/shard_map/add | solution.py:270
  2.8 3.1 %collective-permute-start.2 = (bf16[2,272,128]{2,1,0:T(8,128)(2,1)S(1)}, bf16[2,272,128]{2,1,0:T(8,128)(2,1)S(1)}, u32[]{:S(2)}, u32[]{:S(2)}) collective-permute-start(bf16[2,272,128]{2,1,0:T(8,128)(2,1)S(1)} %pad_maximum_fusion.own), channel_id=1, source_target_pairs={{8,0},{13,1},{10,2},{15,3},{12,4},{9,5},{14,6},{11,7},{0,8},{5,9},... | collective-permute-start | bytes 417800 | tf_op jit(solution)/shard_map/ppermute | solution.py:85
  5.9 2.5 %collective-permute-start.5 = (bf16[272,128]{1,0:T(8,128)(2,1)S(1)}, bf16[272,128]{1,0:T(8,128)(2,1)S(1)}, u32[]{:S(2)}, u32[]{:S(2)}) collective-permute-start(bf16[272,128]{1,0:T(8,128)(2,1)S(1)} %get-tuple-element.14), channel_id=1, source_target_pairs={{16,0},{17,1},{18,2},{19,3},{20,4},{21,5},{22,6},{23,7},{24,8},{25... | collective-permute-start | bytes 208904 | tf_op jit(solution)/shard_map/ppermute | solution.py:85
  8.4 1.5 %collective-permute-start.3 = (bf16[2,272,128]{2,1,0:T(8,128)(2,1)S(1)}, bf16[2,272,128]{2,1,0:T(8,128)(2,1)S(1)}, u32[]{:S(2)}, u32[]{:S(2)}) collective-permute-start(bf16[2,272,128]{2,1,0:T(8,128)(2,1)S(1)} %pad_maximum_fusion.own), channel_id=1, source_target_pairs={{2,0},{7,1},{0,2},{5,3},{6,4},{3,5},{4,6},{1,7},{10,8},{15,9},{8,1... | collective-permute-start | bytes 417800 | tf_op jit(solution)/shard_map/ppermute | solution.py:85
  9.9 1.9 %collective-permute-done.5.c_own = bf16[272,128]{1,0:T(8,128)(2,1)S(1)} collective-permute-done((bf16[272,128]{1,0:T(8,128)(2,1)S(1)}, bf16[272,128]{1,0:T(8,128)(2,1)S(1)}, u32[]{:S(2)}, u32[]{:S(2)}) %collective-permute-start.5) | collective-permute-done | bytes 69664 | tf_op jit(solution)/shard_map/ppermute | solution.py:85
  11.8 0.6 %collective-permute-start.4 = (bf16[272,128]{1,0:T(8,128)(2,1)S(1)}, bf16[272,128]{1,0:T(8,128)(2,1)S(1)}, u32[]{:S(2)}, u32[]{:S(2)}) collective-permute-start(bf16[272,128]{1,0:T(8,128)(2,1)S(1)} %slice_bitcast_fusion), channel_id=1, source_target_pairs={{1,0},{0,1},{3,2},{2,3},{5,4},{4,5},{7,6},{6,7},{9,8},{8,9},{11,10... | collective-permute-start | bytes 208904 | tf_op jit(solution)/shard_map/ppermute | solution.py:85
  12.3 0.7 %collective-permute-done.6.c_other = bf16[272,128]{1,0:T(8,128)(2,1)S(1)} collective-permute-done((bf16[272,128]{1,0:T(8,128)(2,1)S(1)}, bf16[272,128]{1,0:T(8,128)(2,1)S(1)}, u32[]{:S(2)}, u32[]{:S(2)}) %collective-permute-start.6) | collective-permute-done | bytes 69664 | tf_op jit(solution)/shard_map/ppermute | solution.py:85
  13.3 1.3 %shard_map.59 = (f32[256,256]{1,0:T(8,128)S(1)}, f32[2,256]{1,0:T(2,128)S(1)}) custom-call(bf16[2,272,128]{2,1,0:T(8,128)(2,1)S(1)} %pad_maximum_fusion.own, bf16[2,272,128]{2,1,0:T(8,128)(2,1)S(1)} %collective-permute-done.2.a, bf16[272,128]{1,0:T(8,128)(2,1)S(1)} %collective-permute-done.4.e, bf16[272,128]{1,0:T(8,128)(2,1)S(1)} %collective-permute-done.5.c_own, ...), custom_call_target="tpu_custom_call" | custom-call | tf_op jit(solution)/shard_map/pallas_call | solution.py:229
  14.5 1.4 %shard_map.60 = f32[136,256]{1,0:T(8,128)S(1)} custom-call(bf16[2,272,128]{2,1,0:T(8,128)(2,1)S(1)} %pad_maximum_fusion.own, bf16[2,272,128]{2,1,0:T(8,128)(2,1)S(1)} %collective-permute-done.2.a, bf16[2,272,128]{2,1,0:T(8,128)(2,1)S(1)} %collective-permute-done.3.b, bf16[272,128]{1,0:T(8,128)(2,1)S(1)} %collective-permute-done.4.e, ...), custom_call_target="tpu_custom_call" | custom-call | tf_op jit(solution)/shard_map/pallas_call | solution.py:229
  15.9 0.4 %collective-permute-start.7 = (f32[136,256]{1,0:T(8,128)S(1)}, f32[136,256]{1,0:T(8,128)S(1)}, u32[]{:S(2)}, u32[]{:S(2)}) collective-permute-start(f32[136,256]{1,0:T(8,128)S(1)} %shard_map.60), channel_id=1, source_target_pairs={{1,0},{0,1},{3,2},{2,3},{5,4},{4,5},{7,6},{6,7},{9,8},{8,9},{11,10... | collective-permute-start | bytes 417800 | tf_op jit(solution)/shard_map/ppermute | solution.py:85
  16.3 1.0 %collective-permute-done.7 = f32[136,256]{1,0:T(8,128)S(1)} collective-permute-done((f32[136,256]{1,0:T(8,128)S(1)}, f32[136,256]{1,0:T(8,128)S(1)}, u32[]{:S(2)}, u32[]{:S(2)}) %collective-permute-start.7) | collective-permute-done | bytes 139296 | tf_op jit(solution)/shard_map/ppermute | solution.py:85
  17.4 1.7 %collective-permute-start.10 = (bf16[136,256]{1,0:T(8,128)(2,1)S(1)}, bf16[136,256]{1,0:T(8,128)(2,1)S(1)}, u32[]{:S(2)}, u32[]{:S(2)}) collective-permute-start(bf16[136,256]{1,0:T(8,128)(2,1)S(1)} %add_convert_fusion), channel_id=1, source_target_pairs={{16,0},{25,1},{18,2},{27,3},{20,4},{29,5},{22,6},{31,7},{24,8},{17... | collective-permute-start | bytes 208904 | tf_op jit(solution)/shard_map/ppermute | solution.py:85
  19.1 2.9 %collective-permute-start.8 = (bf16[72,256]{1,0:T(8,128)(2,1)S(1)}, bf16[72,256]{1,0:T(8,128)(2,1)S(1)}, u32[]{:S(2)}, u32[]{:S(2)}) collective-permute-start(bf16[72,256]{1,0:T(8,128)(2,1)S(1)} %constant_dynamic-slice_fusion.1), channel_id=1, source_target_pairs={{8,0},{9,1},{10,2},{11,3},{12,4},{13,5},{14,6},{15,7},{0,8},{1,9},... | collective-permute-start | bytes 110600 | tf_op jit(solution)/shard_map/ppermute | solution.py:85
  22.0 1.9 %collective-permute-done.8 = bf16[72,256]{1,0:T(8,128)(2,1)S(1)} collective-permute-done((bf16[72,256]{1,0:T(8,128)(2,1)S(1)}, bf16[72,256]{1,0:T(8,128)(2,1)S(1)}, u32[]{:S(2)}, u32[]{:S(2)}) %collective-permute-start.8) | collective-permute-done | bytes 36896 | tf_op jit(solution)/shard_map/ppermute | solution.py:85
  24.5 0.6 %copy.6 = bf16[2048,256]{0,1:T(8,128)(2,1)S(1)} copy(bf16[2048,256]{1,0:T(8,128)(2,1)S(1)} %copy-done.1) | data formatting | bytes 2097152 | tf_op args[2]
  25.2 0.4 %collective-permute-done.11 = bf16[136,256]{1,0:T(8,128)(2,1)S(1)} collective-permute-done((bf16[136,256]{1,0:T(8,128)(2,1)S(1)}, bf16[136,256]{1,0:T(8,128)(2,1)S(1)}, u32[]{:S(2)}, u32[]{:S(2)}) %collective-permute-start.11) | collective-permute-done | bytes 69664 | tf_op jit(solution)/shard_map/ppermute | solution.py:85
  25.8 1.6 %collective-permute-start.14 = (f16[136,256]{1,0:T(8,128)(2,1)S(1)}, f16[136,256]{1,0:T(8,128)(2,1)S(1)}, u32[]{:S(2)}, u32[]{:S(2)}) collective-permute-start(f16[136,256]{1,0:T(8,128)(2,1)S(1)} %get-tuple-element.11), channel_id=1, source_target_pairs={{4,0},{7,1},{6,2},{5,3},{0,4},{3,5},{2,6},{1,7},{12,8},{15,9},{14,... | collective-permute-start | bytes 208904 | tf_op jit(solution)/shard_map/ppermute | solution.py:85
  27.4 1.5 %collective-permute-start.12 = (f16[72,256]{1,0:T(8,128)(2,1)S(1)}, f16[72,256]{1,0:T(8,128)(2,1)S(1)}, u32[]{:S(2)}, u32[]{:S(2)}) collective-permute-start(f16[72,256]{1,0:T(8,128)(2,1)S(1)} %constant_dynamic-slice_fusion), channel_id=1, source_target_pairs={{2,0},{3,1},{0,2},{1,3},{6,4},{7,5},{4,6},{5,7},{10,8},{11,9},{8,1... | collective-permute-start | bytes 110600 | tf_op jit(solution)/shard_map/ppermute | solution.py:85
  29.0 2.7 %collective-permute-done.12 = f16[72,256]{1,0:T(8,128)(2,1)S(1)} collective-permute-done((f16[72,256]{1,0:T(8,128)(2,1)S(1)}, f16[72,256]{1,0:T(8,128)(2,1)S(1)}, u32[]{:S(2)}, u32[]{:S(2)}) %collective-permute-start.12) | collective-permute-done | bytes 36896 | tf_op jit(solution)/shard_map/ppermute | solution.py:85
  31.9 0.5 %collective-permute-start.15 = (f16[136,256]{1,0:T(8,128)(2,1)S(1)}, f16[136,256]{1,0:T(8,128)(2,1)S(1)}, u32[]{:S(2)}, u32[]{:S(2)}) collective-permute-start(f16[136,256]{1,0:T(8,128)(2,1)S(1)} %collective-permute-done.14), channel_id=1, source_target_pairs={{1,0},{0,1},{3,2},{2,3},{5,4},{4,5},{7,6},{6,7},{9,8},{8,9},{11,10... | collective-permute-start | bytes 208904 | tf_op jit(solution)/shard_map/ppermute | solution.py:85
  32.4 0.6 %collective-permute-done.13 = f16[72,256]{1,0:T(8,128)(2,1)S(1)} collective-permute-done((f16[72,256]{1,0:T(8,128)(2,1)S(1)}, f16[72,256]{1,0:T(8,128)(2,1)S(1)}, u32[]{:S(2)}, u32[]{:S(2)}) %collective-permute-start.13) | collective-permute-done | bytes 36896 | tf_op jit(solution)/shard_map/ppermute | solution.py:85
  33.4 1.3 %shard_map.61 = (f32[1,2048]{1,0:T(1,128)}, f32[256,256]{1,0:T(8,128)}) custom-call(f32[136,256]{1,0:T(8,128)S(1)} %add_add_fusion.total, f32[2,256]{1,0:T(2,128)S(1)} %get-tuple-element.7.gains, bf16[256,2048]{1,0:T(8,128)(2,1)S(1)} %bitcast.14), custom_call_target="tpu_custom_call" | custom-call | tf_op jit(solution)/shard_map/pallas_call | solution.py:229
  (41 shorter events, 1.8 us)
Async XLA Ops:
  0.6 2.1 %collective-permute-start.1 = (s32[3,128]{1,0:T(4,128)}, s32[3,128]{1,0:T(4,128)S(1)}, u32[]{:S(2)}, u32[]{:S(2)}) collective-permute-start(s32[3,128]{1,0:T(4,128)} %param.4), channel_id=1, source_target_pairs={{1,0},{0,1},{3,2},{2,3},{5,4},{4,5},{7,6},{6,7},{9,8},{8,9},{11,10... | collective-permute-start | bytes 4616 | tf_op jit(solution)/shard_map/ppermute | solution.py:85
  1.1 1.7 %collective-permute-start = (bf16[256,128]{1,0:T(8,128)(2,1)}, bf16[256,128]{1,0:T(8,128)(2,1)S(1)}, u32[]{:S(2)}, u32[]{:S(2)}) collective-permute-start(bf16[256,128]{1,0:T(8,128)(2,1)} %param.5), channel_id=1, source_target_pairs={{1,0},{0,1},{3,2},{2,3},{5,4},{4,5},{7,6},{6,7},{9,8},{8,9},{11,10... | collective-permute-start | bytes 196616 | tf_op jit(solution)/shard_map/ppermute | solution.py:85
  2.8 8.9 %collective-permute-start.2 = (bf16[2,272,128]{2,1,0:T(8,128)(2,1)S(1)}, bf16[2,272,128]{2,1,0:T(8,128)(2,1)S(1)}, u32[]{:S(2)}, u32[]{:S(2)}) collective-permute-start(bf16[2,272,128]{2,1,0:T(8,128)(2,1)S(1)} %pad_maximum_fusion.own), channel_id=1, source_target_pairs={{8,0},{13,1},{10,2},{15,3},{12,4},{9,5},{14,6},{11,7},{0,8},{5,9},... | collective-permute-start | bytes 417800 | tf_op jit(solution)/shard_map/ppermute | solution.py:85
  5.9 7.3 %copy-start = (f32[2,256]{1,0:T(2,128)S(1)}, f32[2,256]{1,0:T(2,128)}, u32[]{:S(2)}) copy-start(f32[2,256]{1,0:T(2,128)} %response_gain.1) | copy-start | bytes 6148
  5.9 18.6 %copy-start.1 = (bf16[2048,256]{1,0:T(8,128)(2,1)S(1)}, bf16[2048,256]{1,0:T(8,128)(2,1)}, u32[]{:S(2)}) copy-start(bf16[2048,256]{1,0:T(8,128)(2,1)} %param.6) | copy-start | bytes 3145732
  5.9 5.8 %collective-permute-start.5 = (bf16[272,128]{1,0:T(8,128)(2,1)S(1)}, bf16[272,128]{1,0:T(8,128)(2,1)S(1)}, u32[]{:S(2)}, u32[]{:S(2)}) collective-permute-start(bf16[272,128]{1,0:T(8,128)(2,1)S(1)} %get-tuple-element.14), channel_id=1, source_target_pairs={{16,0},{17,1},{18,2},{19,3},{20,4},{21,5},{22,6},{23,7},{24,8},{25... | collective-permute-start | bytes 208904 | tf_op jit(solution)/shard_map/ppermute | solution.py:85
  8.4 6.1 %collective-permute-start.3 = (bf16[2,272,128]{2,1,0:T(8,128)(2,1)S(1)}, bf16[2,272,128]{2,1,0:T(8,128)(2,1)S(1)}, u32[]{:S(2)}, u32[]{:S(2)}) collective-permute-start(bf16[2,272,128]{2,1,0:T(8,128)(2,1)S(1)} %pad_maximum_fusion.own), channel_id=1, source_target_pairs={{2,0},{7,1},{0,2},{5,3},{6,4},{3,5},{4,6},{1,7},{10,8},{15,9},{8,1... | collective-permute-start | bytes 417800 | tf_op jit(solution)/shard_map/ppermute | solution.py:85
  11.8 1.3 %collective-permute-start.6 = (bf16[272,128]{1,0:T(8,128)(2,1)S(1)}, bf16[272,128]{1,0:T(8,128)(2,1)S(1)}, u32[]{:S(2)}, u32[]{:S(2)}) collective-permute-start(bf16[272,128]{1,0:T(8,128)(2,1)S(1)} %collective-permute-done.5.c_own), channel_id=1, source_target_pairs={{1,0},{0,1},{3,2},{2,3},{5,4},{4,5},{7,6},{6,7},{9,8},{8,9},{11,10... | collective-permute-start | bytes 208904 | tf_op jit(solution)/shard_map/ppermute | solution.py:85
  11.8 1.5 %collective-permute-start.4 = (bf16[272,128]{1,0:T(8,128)(2,1)S(1)}, bf16[272,128]{1,0:T(8,128)(2,1)S(1)}, u32[]{:S(2)}, u32[]{:S(2)}) collective-permute-start(bf16[272,128]{1,0:T(8,128)(2,1)S(1)} %slice_bitcast_fusion), channel_id=1, source_target_pairs={{1,0},{0,1},{3,2},{2,3},{5,4},{4,5},{7,6},{6,7},{9,8},{8,9},{11,10... | collective-permute-start | bytes 208904 | tf_op jit(solution)/shard_map/ppermute | solution.py:85
  15.9 1.4 %collective-permute-start.7 = (f32[136,256]{1,0:T(8,128)S(1)}, f32[136,256]{1,0:T(8,128)S(1)}, u32[]{:S(2)}, u32[]{:S(2)}) collective-permute-start(f32[136,256]{1,0:T(8,128)S(1)} %shard_map.60), channel_id=1, source_target_pairs={{1,0},{0,1},{3,2},{2,3},{5,4},{4,5},{7,6},{6,7},{9,8},{8,9},{11,10... | collective-permute-start | bytes 417800 | tf_op jit(solution)/shard_map/ppermute | solution.py:85
  17.4 7.0 %collective-permute-start.10 = (bf16[136,256]{1,0:T(8,128)(2,1)S(1)}, bf16[136,256]{1,0:T(8,128)(2,1)S(1)}, u32[]{:S(2)}, u32[]{:S(2)}) collective-permute-start(bf16[136,256]{1,0:T(8,128)(2,1)S(1)} %add_convert_fusion), channel_id=1, source_target_pairs={{16,0},{25,1},{18,2},{27,3},{20,4},{29,5},{22,6},{31,7},{24,8},{17... | collective-permute-start | bytes 208904 | tf_op jit(solution)/shard_map/ppermute | solution.py:85
  19.1 4.9 %collective-permute-start.8 = (bf16[72,256]{1,0:T(8,128)(2,1)S(1)}, bf16[72,256]{1,0:T(8,128)(2,1)S(1)}, u32[]{:S(2)}, u32[]{:S(2)}) collective-permute-start(bf16[72,256]{1,0:T(8,128)(2,1)S(1)} %constant_dynamic-slice_fusion.1), channel_id=1, source_target_pairs={{8,0},{9,1},{10,2},{11,3},{12,4},{13,5},{14,6},{15,7},{0,8},{1,9},... | collective-permute-start | bytes 110600 | tf_op jit(solution)/shard_map/ppermute | solution.py:85
  24.0 1.3 %collective-permute-start.9 = (bf16[72,256]{1,0:T(8,128)(2,1)S(1)}, bf16[72,256]{1,0:T(8,128)(2,1)S(1)}, u32[]{:S(2)}, u32[]{:S(2)}) collective-permute-start(bf16[72,256]{1,0:T(8,128)(2,1)S(1)} %collective-permute-done.8), channel_id=1, source_target_pairs={{1,0},{0,1},{3,2},{2,3},{5,4},{4,5},{7,6},{6,7},{9,8},{8,9},{11,10... | collective-permute-start | bytes 110600 | tf_op jit(solution)/shard_map/ppermute | solution.py:85
  24.3 1.3 %collective-permute-start.11 = (bf16[136,256]{1,0:T(8,128)(2,1)S(1)}, bf16[136,256]{1,0:T(8,128)(2,1)S(1)}, u32[]{:S(2)}, u32[]{:S(2)}) collective-permute-start(bf16[136,256]{1,0:T(8,128)(2,1)S(1)} %collective-permute-done.10), channel_id=1, source_target_pairs={{1,0},{0,1},{3,2},{2,3},{5,4},{4,5},{7,6},{6,7},{9,8},{8,9},{11,10... | collective-permute-start | bytes 208904 | tf_op jit(solution)/shard_map/ppermute | solution.py:85
  25.8 6.1 %collective-permute-start.14 = (f16[136,256]{1,0:T(8,128)(2,1)S(1)}, f16[136,256]{1,0:T(8,128)(2,1)S(1)}, u32[]{:S(2)}, u32[]{:S(2)}) collective-permute-start(f16[136,256]{1,0:T(8,128)(2,1)S(1)} %get-tuple-element.11), channel_id=1, source_target_pairs={{4,0},{7,1},{6,2},{5,3},{0,4},{3,5},{2,6},{1,7},{12,8},{15,9},{14,... | collective-permute-start | bytes 208904 | tf_op jit(solution)/shard_map/ppermute | solution.py:85
  27.4 4.3 %collective-permute-start.12 = (f16[72,256]{1,0:T(8,128)(2,1)S(1)}, f16[72,256]{1,0:T(8,128)(2,1)S(1)}, u32[]{:S(2)}, u32[]{:S(2)}) collective-permute-start(f16[72,256]{1,0:T(8,128)(2,1)S(1)} %constant_dynamic-slice_fusion), channel_id=1, source_target_pairs={{2,0},{3,1},{0,2},{1,3},{6,4},{7,5},{4,6},{5,7},{10,8},{11,9},{8,1... | collective-permute-start | bytes 110600 | tf_op jit(solution)/shard_map/ppermute | solution.py:85
  31.7 1.3 %collective-permute-start.13 = (f16[72,256]{1,0:T(8,128)(2,1)S(1)}, f16[72,256]{1,0:T(8,128)(2,1)S(1)}, u32[]{:S(2)}, u32[]{:S(2)}) collective-permute-start(f16[72,256]{1,0:T(8,128)(2,1)S(1)} %collective-permute-done.12), channel_id=1, source_target_pairs={{1,0},{0,1},{3,2},{2,3},{5,4},{4,5},{7,6},{6,7},{9,8},{8,9},{11,10... | collective-permute-start | bytes 110600 | tf_op jit(solution)/shard_map/ppermute | solution.py:85
  31.9 1.4 %collective-permute-start.15 = (f16[136,256]{1,0:T(8,128)(2,1)S(1)}, f16[136,256]{1,0:T(8,128)(2,1)S(1)}, u32[]{:S(2)}, u32[]{:S(2)}) collective-permute-start(f16[136,256]{1,0:T(8,128)(2,1)S(1)} %collective-permute-done.14), channel_id=1, source_target_pairs={{1,0},{0,1},{3,2},{2,3},{5,4},{4,5},{7,6},{6,7},{9,8},{8,9},{11,10... | collective-permute-start | bytes 208904 | tf_op jit(solution)/shard_map/ppermute | solution.py:85

commit v4 on v3

--- a/solution.py
+++ b/solution.py
@@ -71,9 +71,32 @@
 
 
 BIT_X, BIT_Y, BIT_Z, BIT_W = 1, 2, 4, 8
-OFFSET_A = (4, 6)
-OFFSET_B = (1, 3)
-OFFSET_C = (8, 12)
+CHIP_AT = (2, 0, 14, 12, 4, 6, 9, 8, 3, 1, 15, 13, 5, 7, 11, 10)
+OFFSET_A = ((0, 1), (1, 0))
+OFFSET_B = ((4, 0), (6, 1))
+
+
+def moved(place, offset):
+    return (place[0] + offset[0]) % 8, (place[1] + offset[1]) % 2
+
+
+def partner(chip, offset):
+    place = CHIP_AT.index(chip)
+    i, j = moved((place // 2, place % 2), offset)
+    return CHIP_AT[2 * i + j]
+
+
+def share(left, right):
+    shares = []
+    for l, r in zip(left, right):
+        difference = (r[0] - l[0]) % 8, (r[1] - l[1]) % 2
+        shares.append(0.5 if moved(difference, difference) == (0, 0) else 1.0)
+    return tuple(shares)
+
+
+ROLE_S = ((0, 0), (0, 0))
+assert share(ROLE_S, OFFSET_A) == share(ROLE_S, OFFSET_B) == share(OFFSET_A, OFFSET_B)
+assert share(OFFSET_A, OFFSET_A[::-1]) == share(OFFSET_A[::-1], OFFSET_B) == (1.0, 1.0)
 
 
 def receive(array, source):
@@ -136,55 +159,43 @@
     return block[0:256, :]
 
 
-def quarter(left_block, right_block):
-    tile = coherence_tile(left_points(left_block), right_points(right_block))
-    return dot(shapes_of(left_block), tile).astype(jnp.bfloat16), shapes_of(right_block)
-
-
-def full_pair(left_halves, right_halves):
-    lefts = [left_points(h) for h in left_halves]
-    rights = [right_points(h) for h in right_halves]
-    shapes = beside(*[shapes_of(h) for h in left_halves])
-    projections = []
-    for right in rights:
-        column = jnp.concatenate([coherence_tile(left, right) for left in lefts], axis=0)
-        projections.append(dot(shapes, column).astype(jnp.bfloat16))
-    return dot_t(beside(*projections), beside(*[shapes_of(h) for h in right_halves]))
-
-
-def paired(jobs):
-    projections, shapes = zip(*jobs)
-    return dot_t(beside(*projections), beside(*shapes))
-
-
-def upper_bits(*roles):
-    row, col = lax.axis_index("row"), lax.axis_index("col")
-    core, chip = col & 1, row * 2 + (col >> 1)
-    found = []
-    for left_0, left_1, right_0, right_1 in roles:
-        shift_0, shift_1 = ((d & -d).bit_length() - 1 for d in (left_0 ^ right_0, left_1 ^ right_1))
-        on_0, on_1 = ((chip ^ left_0) >> shift_0) & 1, ((chip ^ left_1) >> shift_1) & 1
-        found.append(jnp.where(core == 0, on_0, on_1))
-    return found
-
-
-ROLE_S, ROLE_A, ROLE_B, ROLE_E = (0, 0), OFFSET_A, OFFSET_B, OFFSET_A[::-1]
-
-
-def early_kernel(own, a, e, c_own, c_other, response_gain, out, gains):
+def projection(left_halves, right_half):
+    right = right_points(right_half)
+    tiles = [coherence_tile(left_points(half), right) for half in left_halves]
+    return dot(beside(*[shapes_of(half) for half in left_halves]), jnp.concatenate(tiles, axis=0))
+
+
+def modal(projections, right_halves):
+    return dot_t(
+        beside(*[p.astype(jnp.bfloat16) for p in projections]), beside(*[shapes_of(half) for half in right_halves])
+    )
+
+
+def this_core():
+    return lax.axis_index("col") & 1
+
+
+def own_share():
+    on_0, on_1 = share(ROLE_S, OFFSET_A)
+    return jnp.where(this_core() == 0, on_0, on_1).astype(jnp.float32)
+
+
+def early_kernel(own, a, response_gain, out, gains):
     gains[...] = response_gain[...]
-    sa, ea = upper_bits(ROLE_S + ROLE_A, ROLE_E + ROLE_A)
-    total = paired([quarter(own[0], a[1]), quarter(own[sa], a[sa]), quarter(e[...], a[ea])])
-    total += full_pair([a[0], a[1]], [c_own[...], c_other[...]])
-    total += 0.5 * full_pair([own[0], own[1]], [own[0]])
-    out[...] = total
-
-
-def late_kernel(own, a, b, e, c_own, c_other, early, out):
-    sb, ab, eb = upper_bits(ROLE_S + ROLE_B, ROLE_A + ROLE_B, ROLE_E + ROLE_B)
-    total = early[...]
-    total += full_pair([b[0], b[1]], [c_own[...], c_other[...]])
-    total += paired([quarter(own[0], b[1]), quarter(own[sb], b[sb]), quarter(a[0], b[ab]), quarter(e[...], b[eb])])
+    weight = own_share()
+    pairs = [weight * projection([own[0], own[1]], a[k]) for k in range(2)]
+    pairs.append(0.5 * projection([own[0], own[1]], own[0]))
+    out[...] = modal(pairs, [a[0], a[1], own[0]])
+
+
+def late_kernel(own, a, b, e0, e1, early, out):
+    weight = own_share()
+    pairs = [
+        weight * projection([own[0], own[1], a[0], a[1]], b[k]) + projection([e0[...], e1[...]], b[k]) for k in range(2)
+    ]
+    core = this_core()
+    pairs += [projection([a[core]], e0[...]), projection([a[1 - core]], e1[...])]
+    total = early[...] + modal(pairs, [b[0], b[1], e0[...], e1[...]])
     first = total[0:128, 0:128] + total[0:128, 0:128].T
     second = total[128:256, 128:256] + total[128:256, 128:256].T
     cross = total[0:128, 128:256] + total[128:256, 0:128].T
@@ -277,16 +288,14 @@
     modes, nodes = mode_shapes.shape
     packed = pack(mode_shapes, coords)
     own = jnp.stack([packed, pack(other_core(mode_shapes), other_core(coords))])
-    c_own = receive(packed, lambda chip, c: (chip ^ OFFSET_C[0 if chip < BIT_W else 1], c))
-    a = receive(own, lambda chip, c: (chip ^ OFFSET_A[c], c))
-    b = receive(own, lambda chip, c: (chip ^ OFFSET_B[c], c))
-    c_other = other_core(c_own)
-    e = other_core(a[1])
+    a = receive(own, lambda chip, c: (partner(chip, OFFSET_A[c]), c))
+    b = receive(own, lambda chip, c: (partner(chip, OFFSET_B[c]), c))
+    e0, e1 = other_core(a[0]), other_core(a[1])
     square = jax.ShapeDtypeStruct((modes, modes), jnp.float32)
     tri = jax.ShapeDtypeStruct((modes // 2 + 8, modes), jnp.float32)
     gain_rows = jax.ShapeDtypeStruct(response_gain.shape, jnp.float32)
-    early, gains = call(early_kernel, [VMEM] * 6, [square, gain_rows], own, a, e, c_own, c_other, response_gain)
-    mine = call(late_kernel, [VMEM] * 7, [tri], own, a, b, e, c_own, c_other, early)
+    early, gains = call(early_kernel, [VMEM] * 3, [square, gain_rows], own, a, response_gain)
+    mine = call(late_kernel, [VMEM] * 6, [tri], own, a, b, e0, e1, early)
     chip_sum = mine + other_core(mine)
     f = jnp.float32
     sent = chip_sum.astype(jnp.bfloat16)

time: 34.8 us -> 33.4 us (0.960)
  waiting for transfers between devices: 9.75 us -> 7.99 us
    ppermute x16 -> x15, waiting for transfers between devices: 9.75 us -> 7.99 us  [receive(): return lax.ppermute(array, axes, pairs)]
    add x1 -> x0, other arithmetic: 0.86 us -> none  [pack(): jnp.pad(mode_shapes, ((0, POINT_ROWS), (0, 0)))]
    another operation x2 -> x3, other arithmetic: 0.02 us -> 0.87 us  [local_chips(): own = jnp.stack([packed, pack(other_core(mode_shapes), other_core(coords))])]
    ppermute x16 -> x15, starting transfers between devices: 17.6 us -> 17.9 us  [receive(): return lax.ppermute(array, axes, pairs)]
  transfers between devices with their start and end apart: 16 -> 15, of which waited for: 10 -> 8; matrix products, arithmetic and copies ran while one was open for 7% -> 7% of each run, Pallas kernels for 4% -> 3%
where the time goes in v4:
time: 33.4 us; the launch traced here: 33.2 us
  starting transfers between devices  17.9 us (54%)
  waiting for transfers between devices  7.99 us (24%)
  Pallas kernels  3.92 us (12%)
  other arithmetic  1.89 us (6%)
  between operations  0.79 us (2%)
  local copies, waits for them, and re-layouts  0.71 us (2%)
    ppermute x15, starting transfers between devices, receive(): return lax.ppermute(array, axes, pairs)  17.9 us
    ppermute x15, waiting for transfers between devices, receive(): return lax.ppermute(array, axes, pairs)  7.99 us
    pallas_call x3, Pallas kernels, call(): pl.pallas_call(kernel, in_specs=specs, out_specs=[VMEM] * len(outs) if le...  3.92 us
    another operation x3, other arithmetic, local_chips(): own = jnp.stack([packed, pack(other_core(mode_shapes), other_core(coords))])  0.87 us
    convert_element_type x2, other arithmetic, pack(): (coords >> 8).astype(jnp.bfloat16)  0.69 us
  transfers between devices with their start and end apart: 15, of which 8 were waited for; matrix products, arithmetic and copies ran while one was open for 7% of the time, Pallas kernels for 3%

profile of v4, /device:TPU:0, one launch (start us, length us, event | category | flops | bytes accessed | tf_op | source)
XLA Modules:
  0.0 33.2 jit_solution(14825431227287734373)
XLA Ops:
  0.6 0.5 %collective-permute-start.1 = (s32[3,128]{1,0:T(4,128)}, s32[3,128]{1,0:T(4,128)S(1)}, u32[]{:S(2)}, u32[]{:S(2)}) collective-permute-start(s32[3,128]{1,0:T(4,128)} %param.4), channel_id=1, source_target_pairs={{1,0},{0,1},{3,2},{2,3},{5,4},{4,5},{7,6},{6,7},{9,8},{8,9},{11,10... | collective-permute-start | bytes 4616 | tf_op jit(solution)/shard_map/ppermute | solution.py:108
  1.2 0.7 %shift-right-arithmetic_convert_fusion.1 = (bf16[3,128]{1,0:T(4,128)(2,1)S(1)}, bf16[3,128]{1,0:T(4,128)(2,1)S(1)}) fusion(s32[3,128]{1,0:T(4,128)} %param.4), kind=kLoop, calls=%fused_computation.15 | loop fusion | flops 1536 | bytes 3072 | tf_op jit(solution)/shard_map/convert_element_type | solution.py:279
  1.9 0.8 %add_bitcast_fusion.1 = bf16[1,272,128]{2,1,0:T(8,128)(2,1)S(1)} fusion(bf16[3,128]{1,0:T(4,128)(2,1)S(1)} %get-tuple-element.17, bf16[3,128]{1,0:T(4,128)(2,1)S(1)} %get-tuple-element.16, bf16[256,128]{1,0:T(8,128)(2,1)} %param.5), kind=kLoop, calls=%fused_computation.11 | loop fusion | flops 208896 | bytes 136704 | tf_op jit(solution)/shard_map/stack | solution.py:290
  2.8 3.0 %collective-permute-start.2 = (bf16[2,272,128]{2,1,0:T(8,128)(2,1)S(1)}, bf16[2,272,128]{2,1,0:T(8,128)(2,1)S(1)}, u32[]{:S(2)}, u32[]{:S(2)}) collective-permute-start(bf16[2,272,128]{2,1,0:T(8,128)(2,1)S(1)} %pad_maximum_fusion.own), channel_id=1, source_target_pairs={{4,0},{25,1},{6,2},{27,3},{0,4},{29,5},{2,6},{31,7},{12,8},{19,9},... | collective-permute-start | bytes 417800 | tf_op jit(solution)/shard_map/ppermute | solution.py:108
  5.8 1.5 %collective-permute-start.3 = (bf16[2,272,128]{2,1,0:T(8,128)(2,1)S(1)}, bf16[2,272,128]{2,1,0:T(8,128)(2,1)S(1)}, u32[]{:S(2)}, u32[]{:S(2)}) collective-permute-start(bf16[2,272,128]{2,1,0:T(8,128)(2,1)S(1)} %pad_maximum_fusion.own), channel_id=1, source_target_pairs={{2,0},{11,1},{0,2},{9,3},{6,4},{15,5},{4,6},{13,7},{10,8},{1,9},{8... | collective-permute-start | bytes 417800 | tf_op jit(solution)/shard_map/ppermute | solution.py:108
  7.3 1.5 %collective-permute-done.2.a = bf16[2,272,128]{2,1,0:T(8,128)(2,1)S(1)} collective-permute-done((bf16[2,272,128]{2,1,0:T(8,128)(2,1)S(1)}, bf16[2,272,128]{2,1,0:T(8,128)(2,1)S(1)}, u32[]{:S(2)}, u32[]{:S(2)}) %collective-permute-start.2) | collective-permute-done | bytes 139296 | tf_op jit(solution)/shard_map/ppermute | solution.py:108
  8.9 1.5 %collective-permute-start.5 = (bf16[272,128]{1,0:T(8,128)(2,1)S(1)}, bf16[272,128]{1,0:T(8,128)(2,1)S(1)}, u32[]{:S(2)}, u32[]{:S(2)}) collective-permute-start(bf16[272,128]{1,0:T(8,128)(2,1)S(1)} %get-tuple-element.14), channel_id=1, source_target_pairs={{1,0},{0,1},{3,2},{2,3},{5,4},{4,5},{7,6},{6,7},{9,8},{8,9},{11,10... | collective-permute-start | bytes 208904 | tf_op jit(solution)/shard_map/ppermute | solution.py:108
  10.5 0.9 %shard_map.59 = (f32[256,256]{1,0:T(8,128)S(1)}, f32[2,256]{1,0:T(2,128)S(1)}) custom-call(bf16[2,272,128]{2,1,0:T(8,128)(2,1)S(1)} %pad_maximum_fusion.own, bf16[2,272,128]{2,1,0:T(8,128)(2,1)S(1)} %collective-permute-done.2.a, f32[2,256]{1,0:T(2,128)S(1)} %copy-done), custom_call_target="tpu_custom_call" | custom-call | tf_op jit(solution)/shard_map/pallas_call | solution.py:240
  11.6 1.7 %shard_map.60 = f32[136,256]{1,0:T(8,128)S(1)} custom-call(bf16[2,272,128]{2,1,0:T(8,128)(2,1)S(1)} %pad_maximum_fusion.own, bf16[2,272,128]{2,1,0:T(8,128)(2,1)S(1)} %collective-permute-done.2.a, bf16[2,272,128]{2,1,0:T(8,128)(2,1)S(1)} %collective-permute-done.3.b, bf16[272,128]{1,0:T(8,128)(2,1)S(1)} %collective-permute-done.4.e0, ...), custom_call_target="tpu_custom_call" | custom-call | tf_op jit(solution)/shard_map/pallas_call | solution.py:240
  13.4 1.1 %collective-permute-start.6 = (f32[136,256]{1,0:T(8,128)S(1)}, f32[136,256]{1,0:T(8,128)S(1)}, u32[]{:S(2)}, u32[]{:S(2)}) collective-permute-start(f32[136,256]{1,0:T(8,128)S(1)} %shard_map.60), channel_id=1, source_target_pairs={{1,0},{0,1},{3,2},{2,3},{5,4},{4,5},{7,6},{6,7},{9,8},{8,9},{11,10... | collective-permute-start | bytes 417800 | tf_op jit(solution)/shard_map/ppermute | solution.py:108
  14.5 1.0 %collective-permute-done.6 = f32[136,256]{1,0:T(8,128)S(1)} collective-permute-done((f32[136,256]{1,0:T(8,128)S(1)}, f32[136,256]{1,0:T(8,128)S(1)}, u32[]{:S(2)}, u32[]{:S(2)}) %collective-permute-start.6) | collective-permute-done | bytes 139296 | tf_op jit(solution)/shard_map/ppermute | solution.py:108
  15.5 2.9 %collective-permute-start.9 = (bf16[136,256]{1,0:T(8,128)(2,1)S(1)}, bf16[136,256]{1,0:T(8,128)(2,1)S(1)}, u32[]{:S(2)}, u32[]{:S(2)}) collective-permute-start(bf16[136,256]{1,0:T(8,128)(2,1)S(1)} %add_convert_fusion), channel_id=1, source_target_pairs={{16,0},{25,1},{18,2},{27,3},{20,4},{29,5},{22,6},{31,7},{24,8},{17... | collective-permute-start | bytes 208904 | tf_op jit(solution)/shard_map/ppermute | solution.py:108
  18.3 3.1 %collective-permute-start.7 = (bf16[72,256]{1,0:T(8,128)(2,1)S(1)}, bf16[72,256]{1,0:T(8,128)(2,1)S(1)}, u32[]{:S(2)}, u32[]{:S(2)}) collective-permute-start(bf16[72,256]{1,0:T(8,128)(2,1)S(1)} %constant_dynamic-slice_fusion.1), channel_id=1, source_target_pairs={{8,0},{9,1},{10,2},{11,3},{12,4},{13,5},{14,6},{15,7},{0,8},{1,9},... | collective-permute-start | bytes 110600 | tf_op jit(solution)/shard_map/ppermute | solution.py:108
  21.4 2.0 %collective-permute-done.7 = bf16[72,256]{1,0:T(8,128)(2,1)S(1)} collective-permute-done((bf16[72,256]{1,0:T(8,128)(2,1)S(1)}, bf16[72,256]{1,0:T(8,128)(2,1)S(1)}, u32[]{:S(2)}, u32[]{:S(2)}) %collective-permute-start.7) | collective-permute-done | bytes 36896 | tf_op jit(solution)/shard_map/ppermute | solution.py:108
  23.6 0.3 collective-permute-start.10
  23.9 0.6 %copy.6 = bf16[2048,256]{0,1:T(8,128)(2,1)S(1)} copy(bf16[2048,256]{1,0:T(8,128)(2,1)S(1)} %copy-done.1) | data formatting | bytes 2097152 | tf_op args[2]
  24.6 0.3 collective-permute-done.10
  25.1 0.6 %collective-permute-start.13 = (f16[136,256]{1,0:T(8,128)(2,1)S(1)}, f16[136,256]{1,0:T(8,128)(2,1)S(1)}, u32[]{:S(2)}, u32[]{:S(2)}) collective-permute-start(f16[136,256]{1,0:T(8,128)(2,1)S(1)} %get-tuple-element.11), channel_id=1, source_target_pairs={{4,0},{7,1},{6,2},{5,3},{0,4},{3,5},{2,6},{1,7},{12,8},{15,9},{14,... | collective-permute-start | bytes 208904 | tf_op jit(solution)/shard_map/ppermute | solution.py:108
  25.6 2.5 %collective-permute-start.11 = (f16[72,256]{1,0:T(8,128)(2,1)S(1)}, f16[72,256]{1,0:T(8,128)(2,1)S(1)}, u32[]{:S(2)}, u32[]{:S(2)}) collective-permute-start(f16[72,256]{1,0:T(8,128)(2,1)S(1)} %constant_dynamic-slice_fusion), channel_id=1, source_target_pairs={{2,0},{3,1},{0,2},{1,3},{6,4},{7,5},{4,6},{5,7},{10,8},{11,9},{8,1... | collective-permute-start | bytes 110600 | tf_op jit(solution)/shard_map/ppermute | solution.py:108
  28.1 1.9 %collective-permute-done.11 = f16[72,256]{1,0:T(8,128)(2,1)S(1)} collective-permute-done((f16[72,256]{1,0:T(8,128)(2,1)S(1)}, f16[72,256]{1,0:T(8,128)(2,1)S(1)}, u32[]{:S(2)}, u32[]{:S(2)}) %collective-permute-start.11) | collective-permute-done | bytes 36896 | tf_op jit(solution)/shard_map/ppermute | solution.py:108
  30.1 0.4 %collective-permute-start.12 = (f16[72,256]{1,0:T(8,128)(2,1)S(1)}, f16[72,256]{1,0:T(8,128)(2,1)S(1)}, u32[]{:S(2)}, u32[]{:S(2)}) collective-permute-start(f16[72,256]{1,0:T(8,128)(2,1)S(1)} %collective-permute-done.11), channel_id=1, source_target_pairs={{1,0},{0,1},{3,2},{2,3},{5,4},{4,5},{7,6},{6,7},{9,8},{8,9},{11,10... | collective-permute-start | bytes 110600 | tf_op jit(solution)/shard_map/ppermute | solution.py:108
  30.7 0.6 %collective-permute-done.12 = f16[72,256]{1,0:T(8,128)(2,1)S(1)} collective-permute-done((f16[72,256]{1,0:T(8,128)(2,1)S(1)}, f16[72,256]{1,0:T(8,128)(2,1)S(1)}, u32[]{:S(2)}, u32[]{:S(2)}) %collective-permute-start.12) | collective-permute-done | bytes 36896 | tf_op jit(solution)/shard_map/ppermute | solution.py:108
  31.4 0.4 %collective-permute-done.14 = f16[136,256]{1,0:T(8,128)(2,1)S(1)} collective-permute-done((f16[136,256]{1,0:T(8,128)(2,1)S(1)}, f16[136,256]{1,0:T(8,128)(2,1)S(1)}, u32[]{:S(2)}, u32[]{:S(2)}) %collective-permute-start.14) | collective-permute-done | bytes 69664 | tf_op jit(solution)/shard_map/ppermute | solution.py:108
  31.9 1.3 %shard_map.61 = (f32[1,2048]{1,0:T(1,128)}, f32[256,256]{1,0:T(8,128)}) custom-call(f32[136,256]{1,0:T(8,128)S(1)} %add_add_fusion.total, f32[2,256]{1,0:T(2,128)S(1)} %get-tuple-element.7.gains, bf16[256,2048]{1,0:T(8,128)(2,1)S(1)} %bitcast.16), custom_call_target="tpu_custom_call" | custom-call | tf_op jit(solution)/shard_map/pallas_call | solution.py:240
  (39 shorter events, 1.4 us)
Async XLA Ops:
  0.6 2.1 %collective-permute-start.1 = (s32[3,128]{1,0:T(4,128)}, s32[3,128]{1,0:T(4,128)S(1)}, u32[]{:S(2)}, u32[]{:S(2)}) collective-permute-start(s32[3,128]{1,0:T(4,128)} %param.4), channel_id=1, source_target_pairs={{1,0},{0,1},{3,2},{2,3},{5,4},{4,5},{7,6},{6,7},{9,8},{8,9},{11,10... | collective-permute-start | bytes 4616 | tf_op jit(solution)/shard_map/ppermute | solution.py:108
  1.1 1.6 %collective-permute-start = (bf16[256,128]{1,0:T(8,128)(2,1)}, bf16[256,128]{1,0:T(8,128)(2,1)S(1)}, u32[]{:S(2)}, u32[]{:S(2)}) collective-permute-start(bf16[256,128]{1,0:T(8,128)(2,1)} %param.5), channel_id=1, source_target_pairs={{1,0},{0,1},{3,2},{2,3},{5,4},{4,5},{7,6},{6,7},{9,8},{8,9},{11,10... | collective-permute-start | bytes 196616 | tf_op jit(solution)/shard_map/ppermute | solution.py:108
  2.8 6.0 %collective-permute-start.2 = (bf16[2,272,128]{2,1,0:T(8,128)(2,1)S(1)}, bf16[2,272,128]{2,1,0:T(8,128)(2,1)S(1)}, u32[]{:S(2)}, u32[]{:S(2)}) collective-permute-start(bf16[2,272,128]{2,1,0:T(8,128)(2,1)S(1)} %pad_maximum_fusion.own), channel_id=1, source_target_pairs={{4,0},{25,1},{6,2},{27,3},{0,4},{29,5},{2,6},{31,7},{12,8},{19,9},... | collective-permute-start | bytes 417800 | tf_op jit(solution)/shard_map/ppermute | solution.py:108
  5.8 5.6 %collective-permute-start.3 = (bf16[2,272,128]{2,1,0:T(8,128)(2,1)S(1)}, bf16[2,272,128]{2,1,0:T(8,128)(2,1)S(1)}, u32[]{:S(2)}, u32[]{:S(2)}) collective-permute-start(bf16[2,272,128]{2,1,0:T(8,128)(2,1)S(1)} %pad_maximum_fusion.own), channel_id=1, source_target_pairs={{2,0},{11,1},{0,2},{9,3},{6,4},{15,5},{4,6},{13,7},{10,8},{1,9},{8... | collective-permute-start | bytes 417800 | tf_op jit(solution)/shard_map/ppermute | solution.py:108
  8.9 1.6 %copy-start = (f32[2,256]{1,0:T(2,128)S(1)}, f32[2,256]{1,0:T(2,128)}, u32[]{:S(2)}) copy-start(f32[2,256]{1,0:T(2,128)} %response_gain.1) | copy-start | bytes 6148
  8.9 15.0 %copy-start.1 = (bf16[2048,256]{1,0:T(8,128)(2,1)S(1)}, bf16[2048,256]{1,0:T(8,128)(2,1)}, u32[]{:S(2)}) copy-start(bf16[2048,256]{1,0:T(8,128)(2,1)} %param.6) | copy-start | bytes 3145732
  8.9 2.5 %collective-permute-start.5 = (bf16[272,128]{1,0:T(8,128)(2,1)S(1)}, bf16[272,128]{1,0:T(8,128)(2,1)S(1)}, u32[]{:S(2)}, u32[]{:S(2)}) collective-permute-start(bf16[272,128]{1,0:T(8,128)(2,1)S(1)} %get-tuple-element.14), channel_id=1, source_target_pairs={{1,0},{0,1},{3,2},{2,3},{5,4},{4,5},{7,6},{6,7},{9,8},{8,9},{11,10... | collective-permute-start | bytes 208904 | tf_op jit(solution)/shard_map/ppermute | solution.py:108
  10.4 1.3 %collective-permute-start.4 = (bf16[272,128]{1,0:T(8,128)(2,1)S(1)}, bf16[272,128]{1,0:T(8,128)(2,1)S(1)}, u32[]{:S(2)}, u32[]{:S(2)}) collective-permute-start(bf16[272,128]{1,0:T(8,128)(2,1)S(1)} %get-tuple-element.15), channel_id=1, source_target_pairs={{1,0},{0,1},{3,2},{2,3},{5,4},{4,5},{7,6},{6,7},{9,8},{8,9},{11,10... | collective-permute-start | bytes 208904 | tf_op jit(solution)/shard_map/ppermute | solution.py:108
  13.4 2.1 %collective-permute-start.6 = (f32[136,256]{1,0:T(8,128)S(1)}, f32[136,256]{1,0:T(8,128)S(1)}, u32[]{:S(2)}, u32[]{:S(2)}) collective-permute-start(f32[136,256]{1,0:T(8,128)S(1)} %shard_map.60), channel_id=1, source_target_pairs={{1,0},{0,1},{3,2},{2,3},{5,4},{4,5},{7,6},{6,7},{9,8},{8,9},{11,10... | collective-permute-start | bytes 417800 | tf_op jit(solution)/shard_map/ppermute | solution.py:108
  15.5 8.1 %collective-permute-start.9 = (bf16[136,256]{1,0:T(8,128)(2,1)S(1)}, bf16[136,256]{1,0:T(8,128)(2,1)S(1)}, u32[]{:S(2)}, u32[]{:S(2)}) collective-permute-start(bf16[136,256]{1,0:T(8,128)(2,1)S(1)} %add_convert_fusion), channel_id=1, source_target_pairs={{16,0},{25,1},{18,2},{27,3},{20,4},{29,5},{22,6},{31,7},{24,8},{17... | collective-permute-start | bytes 208904 | tf_op jit(solution)/shard_map/ppermute | solution.py:108
  18.3 5.0 %collective-permute-start.7 = (bf16[72,256]{1,0:T(8,128)(2,1)S(1)}, bf16[72,256]{1,0:T(8,128)(2,1)S(1)}, u32[]{:S(2)}, u32[]{:S(2)}) collective-permute-start(bf16[72,256]{1,0:T(8,128)(2,1)S(1)} %constant_dynamic-slice_fusion.1), channel_id=1, source_target_pairs={{8,0},{9,1},{10,2},{11,3},{12,4},{13,5},{14,6},{15,7},{0,8},{1,9},... | collective-permute-start | bytes 110600 | tf_op jit(solution)/shard_map/ppermute | solution.py:108
  23.4 1.2 %collective-permute-start.8 = (bf16[72,256]{1,0:T(8,128)(2,1)S(1)}, bf16[72,256]{1,0:T(8,128)(2,1)S(1)}, u32[]{:S(2)}, u32[]{:S(2)}) collective-permute-start(bf16[72,256]{1,0:T(8,128)(2,1)S(1)} %collective-permute-done.7), channel_id=1, source_target_pairs={{1,0},{0,1},{3,2},{2,3},{5,4},{4,5},{7,6},{6,7},{9,8},{8,9},{11,10... | collective-permute-start | bytes 110600 | tf_op jit(solution)/shard_map/ppermute | solution.py:108
  23.6 1.3 %collective-permute-start.10 = (bf16[136,256]{1,0:T(8,128)(2,1)S(1)}, bf16[136,256]{1,0:T(8,128)(2,1)S(1)}, u32[]{:S(2)}, u32[]{:S(2)}) collective-permute-start(bf16[136,256]{1,0:T(8,128)(2,1)S(1)} %collective-permute-done.9), channel_id=1, source_target_pairs={{1,0},{0,1},{3,2},{2,3},{5,4},{4,5},{7,6},{6,7},{9,8},{8,9},{11,10... | collective-permute-start | bytes 208904 | tf_op jit(solution)/shard_map/ppermute | solution.py:108
  25.1 5.4 %collective-permute-start.13 = (f16[136,256]{1,0:T(8,128)(2,1)S(1)}, f16[136,256]{1,0:T(8,128)(2,1)S(1)}, u32[]{:S(2)}, u32[]{:S(2)}) collective-permute-start(f16[136,256]{1,0:T(8,128)(2,1)S(1)} %get-tuple-element.11), channel_id=1, source_target_pairs={{4,0},{7,1},{6,2},{5,3},{0,4},{3,5},{2,6},{1,7},{12,8},{15,9},{14,... | collective-permute-start | bytes 208904 | tf_op jit(solution)/shard_map/ppermute | solution.py:108
  25.6 4.4 %collective-permute-start.11 = (f16[72,256]{1,0:T(8,128)(2,1)S(1)}, f16[72,256]{1,0:T(8,128)(2,1)S(1)}, u32[]{:S(2)}, u32[]{:S(2)}) collective-permute-start(f16[72,256]{1,0:T(8,128)(2,1)S(1)} %constant_dynamic-slice_fusion), channel_id=1, source_target_pairs={{2,0},{3,1},{0,2},{1,3},{6,4},{7,5},{4,6},{5,7},{10,8},{11,9},{8,1... | collective-permute-start | bytes 110600 | tf_op jit(solution)/shard_map/ppermute | solution.py:108
  30.1 1.3 %collective-permute-start.12 = (f16[72,256]{1,0:T(8,128)(2,1)S(1)}, f16[72,256]{1,0:T(8,128)(2,1)S(1)}, u32[]{:S(2)}, u32[]{:S(2)}) collective-permute-start(f16[72,256]{1,0:T(8,128)(2,1)S(1)} %collective-permute-done.11), channel_id=1, source_target_pairs={{1,0},{0,1},{3,2},{2,3},{5,4},{4,5},{7,6},{6,7},{9,8},{8,9},{11,10... | collective-permute-start | bytes 110600 | tf_op jit(solution)/shard_map/ppermute | solution.py:108
  30.5 1.3 %collective-permute-start.14 = (f16[136,256]{1,0:T(8,128)(2,1)S(1)}, f16[136,256]{1,0:T(8,128)(2,1)S(1)}, u32[]{:S(2)}, u32[]{:S(2)}) collective-permute-start(f16[136,256]{1,0:T(8,128)(2,1)S(1)} %collective-permute-done.13), channel_id=1, source_target_pairs={{1,0},{0,1},{3,2},{2,3},{5,4},{4,5},{7,6},{6,7},{9,8},{8,9},{11,10... | collective-permute-start | bytes 208904 | tf_op jit(solution)/shard_map/ppermute | solution.py:108

commit v5 on v4

--- a/solution.py
+++ b/solution.py
@@ -71,9 +71,9 @@
 
 
 BIT_X, BIT_Y, BIT_Z, BIT_W = 1, 2, 4, 8
-CHIP_AT = (2, 0, 14, 12, 4, 6, 9, 8, 3, 1, 15, 13, 5, 7, 11, 10)
-OFFSET_A = ((0, 1), (1, 0))
-OFFSET_B = ((4, 0), (6, 1))
+CHIP_AT = (13, 12, 7, 6, 10, 11, 1, 0, 14, 15, 4, 5, 9, 8, 2, 3)
+OFFSET_A = ((0, 1), (3, 0))
+OFFSET_B = ((2, 0), (4, 1))
 
 
 def moved(place, offset):
@@ -95,8 +95,7 @@
 
 
 ROLE_S = ((0, 0), (0, 0))
-assert share(ROLE_S, OFFSET_A) == share(ROLE_S, OFFSET_B) == share(OFFSET_A, OFFSET_B)
-assert share(OFFSET_A, OFFSET_A[::-1]) == share(OFFSET_A[::-1], OFFSET_B) == (1.0, 1.0)
+ROLE_A, ROLE_B, ROLE_E = OFFSET_A, OFFSET_B, OFFSET_A[::-1]
 
 
 def receive(array, source):
@@ -112,23 +111,23 @@
     return receive(array, lambda chip, core: (chip, 1 - core))
 
 
-def left_points(block):
+def column_points(block):
     rows = block[256 : 256 + POINT_ROWS, :].astype(jnp.float32)
     points = rows[0:8, :] * 256.0 + rows[8:16, :]
     columns = jnp.transpose(points, (1, 0))
     return [columns[:, k : k + 1] for k in range(3)]
 
 
-def right_points(block):
+def row_points(block):
     rows = block[256 : 256 + POINT_ROWS, :].astype(jnp.float32)
     points = rows[0:8, :] * 256.0 + rows[8:16, :]
     return [points[k : k + 1, :] for k in range(3)]
 
 
-def coherence_tile(left, right):
+def coherence_tile(columns, rows):
     squared = None
-    for left_column, right_row in zip(left, right):
-        difference = left_column - right_row
+    for column, row in zip(columns, rows):
+        difference = column - row
         term = difference * difference
         squared = term if squared is None else squared + term
     squared = jnp.maximum(squared, 1e-6)
@@ -160,9 +159,15 @@
 
 
 def projection(left_halves, right_half):
-    right = right_points(right_half)
-    tiles = [coherence_tile(left_points(half), right) for half in left_halves]
+    right = row_points(right_half)
+    tiles = [coherence_tile(column_points(half), right) for half in left_halves]
     return dot(beside(*[shapes_of(half) for half in left_halves]), jnp.concatenate(tiles, axis=0))
+
+
+def projection_t(left_halves, right_half):
+    right = column_points(right_half)
+    tiles = [coherence_tile(right, row_points(half)) for half in left_halves]
+    return dot_t(beside(*[shapes_of(half) for half in left_halves]), beside(*tiles))
 
 
 def modal(projections, right_halves):
@@ -175,26 +180,29 @@
     return lax.axis_index("col") & 1
 
 
-def own_share():
-    on_0, on_1 = share(ROLE_S, OFFSET_A)
-    return jnp.where(this_core() == 0, on_0, on_1).astype(jnp.float32)
+def shared(left, right, value):
+    on_0, on_1 = share(left, right)
+    if on_0 == on_1:
+        return value if on_0 == 1.0 else on_0 * value
+    return jnp.where(this_core() == 0, on_0, on_1).astype(jnp.float32) * value
 
 
 def early_kernel(own, a, response_gain, out, gains):
     gains[...] = response_gain[...]
-    weight = own_share()
-    pairs = [weight * projection([own[0], own[1]], a[k]) for k in range(2)]
+    pairs = [shared(ROLE_S, ROLE_A, projection([own[0], own[1]], a[k])) for k in range(2)]
     pairs.append(0.5 * projection([own[0], own[1]], own[0]))
     out[...] = modal(pairs, [a[0], a[1], own[0]])
 
 
 def late_kernel(own, a, b, e0, e1, early, out):
-    weight = own_share()
     pairs = [
-        weight * projection([own[0], own[1], a[0], a[1]], b[k]) + projection([e0[...], e1[...]], b[k]) for k in range(2)
+        shared(ROLE_S, ROLE_B, projection_t([own[0], own[1]], b[k]))
+        + shared(ROLE_A, ROLE_B, projection_t([a[0], a[1]], b[k]))
+        + shared(ROLE_E, ROLE_B, projection_t([e0[...], e1[...]], b[k]))
+        for k in range(2)
     ]
     core = this_core()
-    pairs += [projection([a[core]], e0[...]), projection([a[1 - core]], e1[...])]
+    pairs += [shared(ROLE_A, ROLE_E, projection_t([a[i]], e)) for i, e in ((core, e0[...]), (1 - core, e1[...]))]
     total = early[...] + modal(pairs, [b[0], b[1], e0[...], e1[...]])
     first = total[0:128, 0:128] + total[0:128, 0:128].T
     second = total[128:256, 128:256] + total[128:256, 128:256].T

time: 33.4 us -> 32.9 us (0.985)
  starting transfers between devices: 17.9 us -> 16.5 us
  waiting for transfers between devices: 7.99 us -> 9.07 us
    ppermute x15, starting transfers between devices: 17.9 us -> 16.5 us  [receive(): return lax.ppermute(array, axes, pairs)]
    ppermute x15, waiting for transfers between devices: 7.99 us -> 9.07 us  [receive(): return lax.ppermute(array, axes, pairs)]
  transfers between devices with their start and end apart: 15 -> 15, of which waited for: 8 -> 9; matrix products, arithmetic and copies ran while one was open for 7% -> 7% of each run, Pallas kernels for 3% -> 3%
where the time goes in v5:
time: 32.9 us; the launch traced here: 32.7 us
  starting transfers between devices  16.5 us (50%)
  waiting for transfers between devices  9.07 us (28%)
  Pallas kernels  3.8 us (12%)
  other arithmetic  1.89 us (6%)
  between operations  0.81 us (2%)
  local copies, waits for them, and re-layouts  0.71 us (2%)
    ppermute x15, starting transfers between devices, receive(): return lax.ppermute(array, axes, pairs)  16.5 us
    ppermute x15, waiting for transfers between devices, receive(): return lax.ppermute(array, axes, pairs)  9.07 us
    pallas_call x3, Pallas kernels, call(): pl.pallas_call(kernel, in_specs=specs, out_specs=[VMEM] * len(outs) if le...  3.8 us
    another operation x3, other arithmetic, local_chips(): own = jnp.stack([packed, pack(other_core(mode_shapes), other_core(coords))])  0.87 us
    convert_element_type x2, other arithmetic, pack(): (coords >> 8).astype(jnp.bfloat16)  0.69 us
  transfers between devices with their start and end apart: 15, of which 9 were waited for; matrix products, arithmetic and copies ran while one was open for 7% of the time, Pallas kernels for 3%

profile of v5, /device:TPU:0, one launch (start us, length us, event | category | flops | bytes accessed | tf_op | source)
XLA Modules:
  0.0 32.7 jit_solution(13860347607970506652)
XLA Ops:
  0.6 0.5 %collective-permute-start.1 = (s32[3,128]{1,0:T(4,128)}, s32[3,128]{1,0:T(4,128)S(1)}, u32[]{:S(2)}, u32[]{:S(2)}) collective-permute-start(s32[3,128]{1,0:T(4,128)} %param.4), channel_id=1, source_target_pairs={{1,0},{0,1},{3,2},{2,3},{5,4},{4,5},{7,6},{6,7},{9,8},{8,9},{11,10... | collective-permute-start | bytes 4616 | tf_op jit(solution)/shard_map/ppermute | solution.py:107
  1.2 0.7 %shift-right-arithmetic_convert_fusion.1 = (bf16[3,128]{1,0:T(4,128)(2,1)S(1)}, bf16[3,128]{1,0:T(4,128)(2,1)S(1)}) fusion(s32[3,128]{1,0:T(4,128)} %param.4), kind=kLoop, calls=%fused_computation.15 | loop fusion | flops 1536 | bytes 3072 | tf_op jit(solution)/shard_map/convert_element_type | solution.py:287
  1.9 0.8 %add_bitcast_fusion.1 = bf16[1,272,128]{2,1,0:T(8,128)(2,1)S(1)} fusion(bf16[3,128]{1,0:T(4,128)(2,1)S(1)} %get-tuple-element.17, bf16[3,128]{1,0:T(4,128)(2,1)S(1)} %get-tuple-element.16, bf16[256,128]{1,0:T(8,128)(2,1)} %param.5), kind=kLoop, calls=%fused_computation.11 | loop fusion | flops 208896 | bytes 136704 | tf_op jit(solution)/shard_map/stack | solution.py:298
  2.8 3.0 %collective-permute-start.2 = (bf16[2,272,128]{2,1,0:T(8,128)(2,1)S(1)}, bf16[2,272,128]{2,1,0:T(8,128)(2,1)S(1)}, u32[]{:S(2)}, u32[]{:S(2)}) collective-permute-start(bf16[2,272,128]{2,1,0:T(8,128)(2,1)S(1)} %pad_maximum_fusion.own), channel_id=1, source_target_pairs={{2,0},{17,1},{0,2},{19,3},{6,4},{21,5},{4,6},{23,7},{10,8},{27,9},... | collective-permute-start | bytes 417800 | tf_op jit(solution)/shard_map/ppermute | solution.py:107
  5.8 2.5 %collective-permute-start.3 = (bf16[2,272,128]{2,1,0:T(8,128)(2,1)S(1)}, bf16[2,272,128]{2,1,0:T(8,128)(2,1)S(1)}, u32[]{:S(2)}, u32[]{:S(2)}) collective-permute-start(bf16[2,272,128]{2,1,0:T(8,128)(2,1)S(1)} %pad_maximum_fusion.own), channel_id=1, source_target_pairs={{10,0},{5,1},{8,2},{7,3},{14,4},{1,5},{12,6},{3,7},{4,8},{13,9},{6... | collective-permute-start | bytes 417800 | tf_op jit(solution)/shard_map/ppermute | solution.py:107
  8.3 0.5 %collective-permute-done.2.a = bf16[2,272,128]{2,1,0:T(8,128)(2,1)S(1)} collective-permute-done((bf16[2,272,128]{2,1,0:T(8,128)(2,1)S(1)}, bf16[2,272,128]{2,1,0:T(8,128)(2,1)S(1)}, u32[]{:S(2)}, u32[]{:S(2)}) %collective-permute-start.2) | collective-permute-done | bytes 139296 | tf_op jit(solution)/shard_map/ppermute | solution.py:107
  8.9 1.0 %collective-permute-start.5 = (bf16[272,128]{1,0:T(8,128)(2,1)S(1)}, bf16[272,128]{1,0:T(8,128)(2,1)S(1)}, u32[]{:S(2)}, u32[]{:S(2)}) collective-permute-start(bf16[272,128]{1,0:T(8,128)(2,1)S(1)} %get-tuple-element.14), channel_id=1, source_target_pairs={{1,0},{0,1},{3,2},{2,3},{5,4},{4,5},{7,6},{6,7},{9,8},{8,9},{11,10... | collective-permute-start | bytes 208904 | tf_op jit(solution)/shard_map/ppermute | solution.py:107
  9.9 0.9 %shard_map.59 = (f32[256,256]{1,0:T(8,128)S(1)}, f32[2,256]{1,0:T(2,128)S(1)}) custom-call(bf16[2,272,128]{2,1,0:T(8,128)(2,1)S(1)} %pad_maximum_fusion.own, bf16[2,272,128]{2,1,0:T(8,128)(2,1)S(1)} %collective-permute-done.2.a, f32[2,256]{1,0:T(2,128)S(1)} %copy-done), custom_call_target="tpu_custom_call" | custom-call | tf_op jit(solution)/shard_map/pallas_call | solution.py:248
  10.9 1.3 %collective-permute-done.3.b = bf16[2,272,128]{2,1,0:T(8,128)(2,1)S(1)} collective-permute-done((bf16[2,272,128]{2,1,0:T(8,128)(2,1)S(1)}, bf16[2,272,128]{2,1,0:T(8,128)(2,1)S(1)}, u32[]{:S(2)}, u32[]{:S(2)}) %collective-permute-start.3) | collective-permute-done | bytes 139296 | tf_op jit(solution)/shard_map/ppermute | solution.py:107
  12.2 1.6 %shard_map.60 = f32[136,256]{1,0:T(8,128)S(1)} custom-call(bf16[2,272,128]{2,1,0:T(8,128)(2,1)S(1)} %pad_maximum_fusion.own, bf16[2,272,128]{2,1,0:T(8,128)(2,1)S(1)} %collective-permute-done.2.a, bf16[2,272,128]{2,1,0:T(8,128)(2,1)S(1)} %collective-permute-done.3.b, bf16[272,128]{1,0:T(8,128)(2,1)S(1)} %collective-permute-done.4.e0, ...), custom_call_target="tpu_custom_call" | custom-call | tf_op jit(solution)/shard_map/pallas_call | solution.py:248
  13.9 1.3 %collective-permute-done.6 = f32[136,256]{1,0:T(8,128)S(1)} collective-permute-done((f32[136,256]{1,0:T(8,128)S(1)}, f32[136,256]{1,0:T(8,128)S(1)}, u32[]{:S(2)}, u32[]{:S(2)}) %collective-permute-start.6) | collective-permute-done | bytes 139296 | tf_op jit(solution)/shard_map/ppermute | solution.py:107
  15.2 1.5 %collective-permute-start.9 = (bf16[136,256]{1,0:T(8,128)(2,1)S(1)}, bf16[136,256]{1,0:T(8,128)(2,1)S(1)}, u32[]{:S(2)}, u32[]{:S(2)}) collective-permute-start(bf16[136,256]{1,0:T(8,128)(2,1)S(1)} %add_convert_fusion), channel_id=1, source_target_pairs={{16,0},{25,1},{18,2},{27,3},{20,4},{29,5},{22,6},{31,7},{24,8},{17... | collective-permute-start | bytes 208904 | tf_op jit(solution)/shard_map/ppermute | solution.py:107
  16.7 4.4 %collective-permute-start.7 = (bf16[72,256]{1,0:T(8,128)(2,1)S(1)}, bf16[72,256]{1,0:T(8,128)(2,1)S(1)}, u32[]{:S(2)}, u32[]{:S(2)}) collective-permute-start(bf16[72,256]{1,0:T(8,128)(2,1)S(1)} %constant_dynamic-slice_fusion.1), channel_id=1, source_target_pairs={{8,0},{9,1},{10,2},{11,3},{12,4},{13,5},{14,6},{15,7},{0,8},{1,9},... | collective-permute-start | bytes 110600 | tf_op jit(solution)/shard_map/ppermute | solution.py:107
  21.2 2.1 %collective-permute-done.7 = bf16[72,256]{1,0:T(8,128)(2,1)S(1)} collective-permute-done((bf16[72,256]{1,0:T(8,128)(2,1)S(1)}, bf16[72,256]{1,0:T(8,128)(2,1)S(1)}, u32[]{:S(2)}, u32[]{:S(2)}) %collective-permute-start.7) | collective-permute-done | bytes 36896 | tf_op jit(solution)/shard_map/ppermute | solution.py:107
  23.3 0.4 %collective-permute-start.10 = (bf16[136,256]{1,0:T(8,128)(2,1)S(1)}, bf16[136,256]{1,0:T(8,128)(2,1)S(1)}, u32[]{:S(2)}, u32[]{:S(2)}) collective-permute-start(bf16[136,256]{1,0:T(8,128)(2,1)S(1)} %collective-permute-done.9), channel_id=1, source_target_pairs={{1,0},{0,1},{3,2},{2,3},{5,4},{4,5},{7,6},{6,7},{9,8},{8,9},{11,10... | collective-permute-start | bytes 208904 | tf_op jit(solution)/shard_map/ppermute | solution.py:107
  23.7 0.6 %copy.6 = bf16[2048,256]{0,1:T(8,128)(2,1)S(1)} copy(bf16[2048,256]{1,0:T(8,128)(2,1)S(1)} %copy-done.1) | data formatting | bytes 2097152 | tf_op args[2]
  24.4 0.2 collective-permute-done.10
  24.8 1.0 %collective-permute-start.13 = (f16[136,256]{1,0:T(8,128)(2,1)S(1)}, f16[136,256]{1,0:T(8,128)(2,1)S(1)}, u32[]{:S(2)}, u32[]{:S(2)}) collective-permute-start(f16[136,256]{1,0:T(8,128)(2,1)S(1)} %get-tuple-element.11), channel_id=1, source_target_pairs={{4,0},{7,1},{6,2},{5,3},{0,4},{3,5},{2,6},{1,7},{12,8},{15,9},{14,... | collective-permute-start | bytes 208904 | tf_op jit(solution)/shard_map/ppermute | solution.py:107
  25.8 1.3 %collective-permute-start.11 = (f16[72,256]{1,0:T(8,128)(2,1)S(1)}, f16[72,256]{1,0:T(8,128)(2,1)S(1)}, u32[]{:S(2)}, u32[]{:S(2)}) collective-permute-start(f16[72,256]{1,0:T(8,128)(2,1)S(1)} %constant_dynamic-slice_fusion), channel_id=1, source_target_pairs={{2,0},{3,1},{0,2},{1,3},{6,4},{7,5},{4,6},{5,7},{10,8},{11,9},{8,1... | collective-permute-start | bytes 110600 | tf_op jit(solution)/shard_map/ppermute | solution.py:107
  27.1 2.7 %collective-permute-done.11 = f16[72,256]{1,0:T(8,128)(2,1)S(1)} collective-permute-done((f16[72,256]{1,0:T(8,128)(2,1)S(1)}, f16[72,256]{1,0:T(8,128)(2,1)S(1)}, u32[]{:S(2)}, u32[]{:S(2)}) %collective-permute-start.11) | collective-permute-done | bytes 36896 | tf_op jit(solution)/shard_map/ppermute | solution.py:107
  30.0 0.5 %collective-permute-start.14 = (f16[136,256]{1,0:T(8,128)(2,1)S(1)}, f16[136,256]{1,0:T(8,128)(2,1)S(1)}, u32[]{:S(2)}, u32[]{:S(2)}) collective-permute-start(f16[136,256]{1,0:T(8,128)(2,1)S(1)} %collective-permute-done.13), channel_id=1, source_target_pairs={{1,0},{0,1},{3,2},{2,3},{5,4},{4,5},{7,6},{6,7},{9,8},{8,9},{11,10... | collective-permute-start | bytes 208904 | tf_op jit(solution)/shard_map/ppermute | solution.py:107
  30.5 0.6 %collective-permute-done.12 = f16[72,256]{1,0:T(8,128)(2,1)S(1)} collective-permute-done((f16[72,256]{1,0:T(8,128)(2,1)S(1)}, f16[72,256]{1,0:T(8,128)(2,1)S(1)}, u32[]{:S(2)}, u32[]{:S(2)}) %collective-permute-start.12) | collective-permute-done | bytes 36896 | tf_op jit(solution)/shard_map/ppermute | solution.py:107
  31.1 0.2 collective-permute-done.14
  31.5 1.3 %shard_map.61 = (f32[1,2048]{1,0:T(1,128)}, f32[256,256]{1,0:T(8,128)}) custom-call(f32[136,256]{1,0:T(8,128)S(1)} %add_add_fusion.total, f32[2,256]{1,0:T(2,128)S(1)} %get-tuple-element.7.gains, bf16[256,2048]{1,0:T(8,128)(2,1)S(1)} %bitcast.16), custom_call_target="tpu_custom_call" | custom-call | tf_op jit(solution)/shard_map/pallas_call | solution.py:248
  (39 shorter events, 1.0 us)
Async XLA Ops:
  0.6 2.1 %collective-permute-start.1 = (s32[3,128]{1,0:T(4,128)}, s32[3,128]{1,0:T(4,128)S(1)}, u32[]{:S(2)}, u32[]{:S(2)}) collective-permute-start(s32[3,128]{1,0:T(4,128)} %param.4), channel_id=1, source_target_pairs={{1,0},{0,1},{3,2},{2,3},{5,4},{4,5},{7,6},{6,7},{9,8},{8,9},{11,10... | collective-permute-start | bytes 4616 | tf_op jit(solution)/shard_map/ppermute | solution.py:107
  1.1 1.6 %collective-permute-start = (bf16[256,128]{1,0:T(8,128)(2,1)}, bf16[256,128]{1,0:T(8,128)(2,1)S(1)}, u32[]{:S(2)}, u32[]{:S(2)}) collective-permute-start(bf16[256,128]{1,0:T(8,128)(2,1)} %param.5), channel_id=1, source_target_pairs={{1,0},{0,1},{3,2},{2,3},{5,4},{4,5},{7,6},{6,7},{9,8},{8,9},{11,10... | collective-permute-start | bytes 196616 | tf_op jit(solution)/shard_map/ppermute | solution.py:107
  2.8 6.0 %collective-permute-start.2 = (bf16[2,272,128]{2,1,0:T(8,128)(2,1)S(1)}, bf16[2,272,128]{2,1,0:T(8,128)(2,1)S(1)}, u32[]{:S(2)}, u32[]{:S(2)}) collective-permute-start(bf16[2,272,128]{2,1,0:T(8,128)(2,1)S(1)} %pad_maximum_fusion.own), channel_id=1, source_target_pairs={{2,0},{17,1},{0,2},{19,3},{6,4},{21,5},{4,6},{23,7},{10,8},{27,9},... | collective-permute-start | bytes 417800 | tf_op jit(solution)/shard_map/ppermute | solution.py:107
  5.8 6.4 %collective-permute-start.3 = (bf16[2,272,128]{2,1,0:T(8,128)(2,1)S(1)}, bf16[2,272,128]{2,1,0:T(8,128)(2,1)S(1)}, u32[]{:S(2)}, u32[]{:S(2)}) collective-permute-start(bf16[2,272,128]{2,1,0:T(8,128)(2,1)S(1)} %pad_maximum_fusion.own), channel_id=1, source_target_pairs={{10,0},{5,1},{8,2},{7,3},{14,4},{1,5},{12,6},{3,7},{4,8},{13,9},{6... | collective-permute-start | bytes 417800 | tf_op jit(solution)/shard_map/ppermute | solution.py:107
  8.8 1.1 %copy-start = (f32[2,256]{1,0:T(2,128)S(1)}, f32[2,256]{1,0:T(2,128)}, u32[]{:S(2)}) copy-start(f32[2,256]{1,0:T(2,128)} %response_gain.1) | copy-start | bytes 6148
  8.9 14.9 %copy-start.1 = (bf16[2048,256]{1,0:T(8,128)(2,1)S(1)}, bf16[2048,256]{1,0:T(8,128)(2,1)}, u32[]{:S(2)}) copy-start(bf16[2048,256]{1,0:T(8,128)(2,1)} %param.6) | copy-start | bytes 3145732
  8.9 3.3 %collective-permute-start.5 = (bf16[272,128]{1,0:T(8,128)(2,1)S(1)}, bf16[272,128]{1,0:T(8,128)(2,1)S(1)}, u32[]{:S(2)}, u32[]{:S(2)}) collective-permute-start(bf16[272,128]{1,0:T(8,128)(2,1)S(1)} %get-tuple-element.14), channel_id=1, source_target_pairs={{1,0},{0,1},{3,2},{2,3},{5,4},{4,5},{7,6},{6,7},{9,8},{8,9},{11,10... | collective-permute-start | bytes 208904 | tf_op jit(solution)/shard_map/ppermute | solution.py:107
  9.9 2.3 %collective-permute-start.4 = (bf16[272,128]{1,0:T(8,128)(2,1)S(1)}, bf16[272,128]{1,0:T(8,128)(2,1)S(1)}, u32[]{:S(2)}, u32[]{:S(2)}) collective-permute-start(bf16[272,128]{1,0:T(8,128)(2,1)S(1)} %get-tuple-element.15), channel_id=1, source_target_pairs={{1,0},{0,1},{3,2},{2,3},{5,4},{4,5},{7,6},{6,7},{9,8},{8,9},{11,10... | collective-permute-start | bytes 208904 | tf_op jit(solution)/shard_map/ppermute | solution.py:107
  13.8 1.4 %collective-permute-start.6 = (f32[136,256]{1,0:T(8,128)S(1)}, f32[136,256]{1,0:T(8,128)S(1)}, u32[]{:S(2)}, u32[]{:S(2)}) collective-permute-start(f32[136,256]{1,0:T(8,128)S(1)} %shard_map.60), channel_id=1, source_target_pairs={{1,0},{0,1},{3,2},{2,3},{5,4},{4,5},{7,6},{6,7},{9,8},{8,9},{11,10... | collective-permute-start | bytes 417800 | tf_op jit(solution)/shard_map/ppermute | solution.py:107
  15.2 8.1 %collective-permute-start.9 = (bf16[136,256]{1,0:T(8,128)(2,1)S(1)}, bf16[136,256]{1,0:T(8,128)(2,1)S(1)}, u32[]{:S(2)}, u32[]{:S(2)}) collective-permute-start(bf16[136,256]{1,0:T(8,128)(2,1)S(1)} %add_convert_fusion), channel_id=1, source_target_pairs={{16,0},{25,1},{18,2},{27,3},{20,4},{29,5},{22,6},{31,7},{24,8},{17... | collective-permute-start | bytes 208904 | tf_op jit(solution)/shard_map/ppermute | solution.py:107
  16.7 6.5 %collective-permute-start.7 = (bf16[72,256]{1,0:T(8,128)(2,1)S(1)}, bf16[72,256]{1,0:T(8,128)(2,1)S(1)}, u32[]{:S(2)}, u32[]{:S(2)}) collective-permute-start(bf16[72,256]{1,0:T(8,128)(2,1)S(1)} %constant_dynamic-slice_fusion.1), channel_id=1, source_target_pairs={{8,0},{9,1},{10,2},{11,3},{12,4},{13,5},{14,6},{15,7},{0,8},{1,9},... | collective-permute-start | bytes 110600 | tf_op jit(solution)/shard_map/ppermute | solution.py:107
  23.2 1.2 %collective-permute-start.8 = (bf16[72,256]{1,0:T(8,128)(2,1)S(1)}, bf16[72,256]{1,0:T(8,128)(2,1)S(1)}, u32[]{:S(2)}, u32[]{:S(2)}) collective-permute-start(bf16[72,256]{1,0:T(8,128)(2,1)S(1)} %collective-permute-done.7), channel_id=1, source_target_pairs={{1,0},{0,1},{3,2},{2,3},{5,4},{4,5},{7,6},{6,7},{9,8},{8,9},{11,10... | collective-permute-start | bytes 110600 | tf_op jit(solution)/shard_map/ppermute | solution.py:107
  23.3 1.3 %collective-permute-start.10 = (bf16[136,256]{1,0:T(8,128)(2,1)S(1)}, bf16[136,256]{1,0:T(8,128)(2,1)S(1)}, u32[]{:S(2)}, u32[]{:S(2)}) collective-permute-start(bf16[136,256]{1,0:T(8,128)(2,1)S(1)} %collective-permute-done.9), channel_id=1, source_target_pairs={{1,0},{0,1},{3,2},{2,3},{5,4},{4,5},{7,6},{6,7},{9,8},{8,9},{11,10... | collective-permute-start | bytes 208904 | tf_op jit(solution)/shard_map/ppermute | solution.py:107
  24.8 5.1 %collective-permute-start.13 = (f16[136,256]{1,0:T(8,128)(2,1)S(1)}, f16[136,256]{1,0:T(8,128)(2,1)S(1)}, u32[]{:S(2)}, u32[]{:S(2)}) collective-permute-start(f16[136,256]{1,0:T(8,128)(2,1)S(1)} %get-tuple-element.11), channel_id=1, source_target_pairs={{4,0},{7,1},{6,2},{5,3},{0,4},{3,5},{2,6},{1,7},{12,8},{15,9},{14,... | collective-permute-start | bytes 208904 | tf_op jit(solution)/shard_map/ppermute | solution.py:107
  25.8 4.0 %collective-permute-start.11 = (f16[72,256]{1,0:T(8,128)(2,1)S(1)}, f16[72,256]{1,0:T(8,128)(2,1)S(1)}, u32[]{:S(2)}, u32[]{:S(2)}) collective-permute-start(f16[72,256]{1,0:T(8,128)(2,1)S(1)} %constant_dynamic-slice_fusion), channel_id=1, source_target_pairs={{2,0},{3,1},{0,2},{1,3},{6,4},{7,5},{4,6},{5,7},{10,8},{11,9},{8,1... | collective-permute-start | bytes 110600 | tf_op jit(solution)/shard_map/ppermute | solution.py:107
  29.8 1.3 %collective-permute-start.12 = (f16[72,256]{1,0:T(8,128)(2,1)S(1)}, f16[72,256]{1,0:T(8,128)(2,1)S(1)}, u32[]{:S(2)}, u32[]{:S(2)}) collective-permute-start(f16[72,256]{1,0:T(8,128)(2,1)S(1)} %collective-permute-done.11), channel_id=1, source_target_pairs={{1,0},{0,1},{3,2},{2,3},{5,4},{4,5},{7,6},{6,7},{9,8},{8,9},{11,10... | collective-permute-start | bytes 110600 | tf_op jit(solution)/shard_map/ppermute | solution.py:107
  30.0 1.4 %collective-permute-start.14 = (f16[136,256]{1,0:T(8,128)(2,1)S(1)}, f16[136,256]{1,0:T(8,128)(2,1)S(1)}, u32[]{:S(2)}, u32[]{:S(2)}) collective-permute-start(f16[136,256]{1,0:T(8,128)(2,1)S(1)} %collective-permute-done.13), channel_id=1, source_target_pairs={{1,0},{0,1},{3,2},{2,3},{5,4},{4,5},{7,6},{6,7},{9,8},{8,9},{11,10... | collective-permute-start | bytes 208904 | tf_op jit(solution)/shard_map/ppermute | solution.py:107
